TPU v7x, 256 devices: a whole 4x4x8 slice. The times are simulated.
256 devices in a mesh: dp: 32 (over x, y, core), vocab: 8 (over z).
Axes of the slice: x: 4, y: 4, z: 8, core: 2. Of those that a mesh axis runs over, the one named last changes fastest.
Arguments:
- student_hidden: bfloat16 [4096, 1536], P('dp'), may hold values from -16 to 16
- head_weight: bfloat16 [1536, 32768], P('dp', 'vocab'), may hold values from -1 to 1
- teacher_logprobs: float32 [4096, 40960], P('dp', 'vocab'), may hold values from -45 to 0, as said below
- align_index: int32 [256, 2], replicated, may hold values from 0 to 319, as said below
- align_tiles: bfloat16 [256, 2, 128, 128], P('vocab'), may hold values from 0 to 6.1
- grad_scale: float32 [4096], P('dp'), may hold values from 30 to 300
Outputs:
- hidden_grad: bfloat16 [4096, 1536], P('dp', 'vocab')
- head_grad: bfloat16 [1536, 32768], P('dp', 'vocab')
Inputs may be any that keep to these rules, and one draw needn't show every extreme that they name: `teacher_logprobs`: each row's exponentials sum to 1 over the 40960 teacher entries. `align_index`: teacher block j is held by vocab index j // 40. Of the 64 entries of the student blocks held by one vocab index, at most 16 name teacher blocks held by any one vocab index, and for every vocab index some vocab index holds exactly 16 of them.
All inputs are finite; a program needn't handle non-finite values.
Results may differ from a plain program's by a relative error of at most 0.015.
Values may be sent and summed in bfloat16 or wider, within the bound.
A program may use at most 128 MiB of HBM per device.

v0:
```python
import jax
import jax.numpy as jnp
from jax import lax
from jax.sharding import PartitionSpec as P

BLOCK = 128
K = 2


def pair_tables(index_rows, teacher_count, vocab_count):
    owner_of = index_rows // teacher_count
    local_block = index_rows % teacher_count
    onehot = (owner_of[..., None] == jnp.arange(vocab_count)[None, None, :]).astype(jnp.int32)
    running = jnp.cumsum(onehot, axis=1)
    slot_rank = jnp.sum(onehot * running, axis=2) - 1
    return (owner_of, local_block, slot_rank)


def body(student_hidden, head_weight, teacher_logprobs, align_index, align_tiles, grad_scale):
    vocab_count = lax.axis_size("vocab")
    own_index = lax.axis_index("vocab")
    tokens_here = student_hidden.shape[0]
    student_cols = head_weight.shape[1]
    student_count = student_cols // BLOCK
    teacher_count = teacher_logprobs.shape[1] // BLOCK
    pair_count = student_count * K
    capacity = (2 * pair_count + vocab_count - 1) // vocab_count
    all_rows = align_index.reshape(vocab_count, pair_count)
    owner_all, local_all, rank_all = pair_tables(all_rows, teacher_count, vocab_count)
    held_here = owner_all == own_index
    slot_numbers = jnp.arange(capacity)
    selected = (
        held_here[:, None, :] & (rank_all[:, None, :] == slot_numbers[None, :, None])
    ).astype(jnp.int32)
    source_block = jnp.sum(selected * local_all[:, None, :], axis=2).reshape(-1)
    filled = jnp.sum(selected, axis=2).reshape(-1) > 0
    teacher_probs = (
        jnp.exp(teacher_logprobs).astype(jnp.bfloat16).reshape(tokens_here, teacher_count, BLOCK)
    )
    outgoing = jnp.take(teacher_probs, source_block, axis=1)
    outgoing = jnp.where(filled[None, :, None], outgoing, jnp.zeros_like(outgoing))
    own_owner = lax.dynamic_index_in_dim(owner_all, own_index, 0, keepdims=False)
    own_rank = lax.dynamic_index_in_dim(rank_all, own_index, 0, keepdims=False)
    where_from = own_owner * capacity + own_rank
    arrived = lax.all_to_all(outgoing, "vocab", split_axis=1, concat_axis=1, tiled=True)
    picked = jnp.take(arrived, where_from, axis=1).reshape(
        arrived.shape[0], student_count, K, BLOCK
    )
    mapped_rows = jnp.einsum(
        "tbkj,bkji->tbi", picked, align_tiles, preferred_element_type=jnp.float32
    )
    mapped = mapped_rows.reshape(arrived.shape[0], student_cols)
    full_weight = lax.all_gather(head_weight, "dp", axis=0, tiled=True)
    logits = jnp.dot(student_hidden, full_weight, preferred_element_type=jnp.float32)
    row_max = lax.pmax(jnp.max(logits, axis=1), "vocab")
    shifted = jnp.exp(logits - row_max[:, None])
    row_total, mass = lax.psum((jnp.sum(shifted, axis=1), jnp.sum(mapped, axis=1)), "vocab")
    student_probs = shifted / row_total[:, None]
    dlogits = (grad_scale[:, None] * (mass[:, None] * student_probs - mapped)).astype(jnp.bfloat16)
    hidden_terms = lax.dot_general(
        dlogits, full_weight, (((1,), (1,)), ((), ())), preferred_element_type=jnp.float32
    )
    hidden_grad = lax.psum_scatter(
        hidden_terms.astype(jnp.bfloat16), "vocab", scatter_dimension=1, tiled=True
    )
    head_grad = lax.psum_scatter(
        lax.dot_general(
            student_hidden, dlogits, (((0,), (0,)), ((), ())), preferred_element_type=jnp.float32
        ).astype(jnp.bfloat16),
        "dp",
        scatter_dimension=0,
        tiled=True,
    )
    return (hidden_grad, head_grad)


def solution(mesh):
    placed = (
        P("dp", None),
        P("dp", "vocab"),
        P("dp", "vocab"),
        P(),
        P("vocab", None, None, None),
        P("dp"),
    )
    return jax.shard_map(
        body,
        mesh=mesh,
        in_specs=placed,
        out_specs=(P("dp", "vocab"), P("dp", "vocab")),
        check_vma=False,
    )
```

profile of v0, /device:TPU:1, one launch (start us, length us, event | category | flops | bytes accessed | tf_op | source)
XLA Modules:
  0.0 348.0 jit_solution(12115876877125369388)
XLA Ops:
  7.2 0.7 all-gather.2.cloned.1.call-update
  7.9 0.7 sign_compare_fusion
  8.6 0.2 copy.83
  8.8 0.1 ne.50
  8.9 0.7 broadcast_remainder_fusion
  9.6 0.1 copy.84
  9.8 0.1 rem.30
  9.9 0.1 copy.85
  10.3 1.3 fusion.13
  11.6 0.4 convert_reduce_fusion
  12.3 3.2 copy.88
  15.5 3.2 exponential_convert_fusion
  18.7 1.8 copy.89
  20.4 3.0 gather_fusion
  23.5 4.1 %select_bitcast_fusion = bf16[128,128,128]{2,0,1:T(8,128)(2,1)} fusion(bf16[128,128,128]{2,1,0:T(8,128)(2,1)} %gather_fusion, pred[128]{0:T(512)(128)(4,1)S(1)} %gt.19, pred[128]{0:T(512)(128)(4,1)S(1)} %compare_and_fusion.1), kind=kLoop, calls=%fused_computation.4 | loop fusion | flops 4194304 | bytes 8388864 | tf_op jit(solution)/shard_map/jit(_where)/select_n | solution.py:41
  27.5 9.2 %all-to-all-start = ((bf16[128,128,128]{2,0,1:T(8,128)(2,1)}), bf16[128,128,128]{2,0,1:T(8,128)(2,1)}, u32[]{:S(2)}, u32[]{:S(2)}) async-start(bf16[128,128,128]{2,0,1:T(8,128)(2,1)} %select_bitcast_fusion), calls=%async_computation | async-start | bytes 8388608 | tf_op jit(solution)/shard_map/all_to_all | solution.py:45
  36.8 0.5 broadcast.185
  37.3 0.7 fusion.12
  38.1 95.5 %all-to-all-done = bf16[128,128,128]{2,0,1:T(8,128)(2,1)} async-done(((bf16[128,128,128]{2,0,1:T(8,128)(2,1)}), bf16[128,128,128]{2,0,1:T(8,128)(2,1)}, u32[]{:S(2)}, u32[]{:S(2)}) %all-to-all-start) | async-done | bytes 4194336 | tf_op jit(solution)/shard_map/all_to_all | solution.py:45
  133.6 4.4 %gather_fusion.1 = bf16[64,128,128]{2,1,0:T(8,128)(2,1)} fusion(bf16[128,128,128]{2,0,1:T(8,128)(2,1)} %all-to-all-done, s32[1024]{0:T(1024)S(1)} %pad_clamp_fusion), kind=kCustom, calls=%fused_computation.1 | custom fusion | bytes 4194560 | tf_op jit(solution)/shard_map/jit(_take)/gather | solution.py:46
  137.9 3.8 %bitcast_reduce_fusion = (f32[128]{0:T(128)S(1)}, f32[32,128,128,1]{1,2,3,0:T(8,128)}) fusion(bf16[32,2,128,128]{3,2,1,0:T(8,128)(2,1)S(1)} %copy-done, bf16[128,32,2,128]{3,0,2,1:T(8,128)(2,1)} %bitcast.27, pred[32,2]{1,0:T(8,128)(4,1)S(1)} %compare_and_fusion), kind=kOutput, calls=%fused_computation.7 | convolution fusion | flops 270008192 | bytes 6292032 | tf_op jit(solution)/shard_map/tbkj,bkji->tbi/dot_general | solution.py:49
  141.7 3.0 copy.91
  144.7 6.5 %fusion.14 = (f32[128]{0:T(128)S(1)}, f32[128,4096]{1,0:T(8,128)S(1)}) fusion(bf16[128,1536]{1,0:T(8,128)(2,1)S(1)} %copy-done.2, bf16[1536,4096]{1,0:T(8,128)(2,1)} %all-gather.2.cloned.1.call-done), kind=kOutput, calls=%fused_computation.46 | convolution fusion | flops 1611136896 | bytes 15073792 | tf_op jit(solution)/shard_map/dot_general | solution.py:54
  151.2 10.9 %pmax.7 = f32[128]{0:T(128)S(1)} all-reduce(f32[128]{0:T(128)S(1)} %get-tuple-element.26), channel_id=1, replica_groups=mesh['dp'=32,'vocab'=8] {'vocab'}, use_global_device_ids=true, to_apply=%region_7.8 | all-reduce | flops 128 | bytes 1024 | tf_op jit(solution)/shard_map/pmax | solution.py:55
  162.1 0.4 fusion.4
  162.5 12.2 %all-reduce = (f32[128]{0:T(128)S(1)}, f32[128]{0:T(128)S(1)}) all-reduce(f32[128]{0:T(128)S(1)} %fusion.4, f32[128]{0:T(128)S(1)} %get-tuple-element.28), channel_id=1, replica_groups=mesh['dp'=32,'vocab'=8] {'vocab'}, use_global_device_ids=true, to_apply=%region_9.10 | all-reduce | flops 256 | bytes 2048 | tf_op jit(solution)/shard_map/psum | solution.py:57
  174.7 9.6 %convolution_convert_fusion.1 = bf16[128,1536]{0,1:T(8,128)(2,1)} fusion(bf16[1536,4096]{1,0:T(8,128)(2,1)} %all-gather.2.cloned.1.call-done, f32[128,4096]{1,0:T(8,128)} %copy.91, f32[128,4096]{1,0:T(8,128)S(1)} %get-tuple-element.27, f32[128]{0:T(128)S(1)} %get-tuple-element.18, f32[128]{0:T(128)S(1)} %pmax.7, f32[128]{0:T(128)S(1)} %get-tuple-element.19, ...), kind=kOutput, calls=%fused_computation.6 | convolution fusion | flops 1613955072 | bytes 17172480 | tf_op jit(solution)/shard_map/dot_general | solution.py:60
  184.4 0.2 reduce-scatter.7.cloned.1.call-start
  184.6 8.7 %fusion = bf16[1536,4096]{0,1:T(8,128)(2,1)} fusion(bf16[128,1536]{1,0:T(8,128)(2,1)S(1)} %copy-done.2, f32[128,4096]{1,0:T(8,128)} %copy.91, f32[128,4096]{1,0:T(8,128)S(1)} %get-tuple-element.27, f32[128]{0:T(128)S(1)} %get-tuple-element.18, f32[128]{0:T(128)S(1)} %pmax.7, f32[128]{0:T(128)S(1)} %get-tuple-element.19, f32[128]{0:T(128)S(1)} %copy-done.3), kind=kOutput, calls=%fused_computation.3 | convolution fusion | flops 1620049920 | bytes 17172480 | tf_op jit(solution)/shard_map/dot_general | solution.py:67
  193.3 16.8 %copy.95 = bf16[1536,4096]{1,0:T(8,128)(2,1)} copy(bf16[1536,4096]{0,1:T(8,128)(2,1)} %fusion) | data formatting | bytes 25165824
  210.1 11.9 %reduce-scatter.5.cloned.1.call-done = bf16[128,192]{0,1:T(8,128)(2,1)} async-done(((bf16[128,1536]{0,1:T(8,128)(2,1)}), bf16[128,192]{0,1:T(8,128)(2,1)}) %reduce-scatter.5.cloned.1.call-update) | async-done | bytes 49168 | tf_op jit(solution)/shard_map/reduce_scatter | solution.py:63
  222.0 119.5 %reduce-scatter.7.cloned.1.call-done = bf16[48,4096]{1,0:T(8,128)(2,1)} async-done(((bf16[1536,4096]{1,0:T(8,128)(2,1)}), bf16[48,4096]{1,0:T(8,128)(2,1)}) %reduce-scatter.7.cloned.1.call-update) | async-done | bytes 393232
  (29 shorter events, 0.8 us)
Async XLA Ops:
  7.2 130.7 %copy-start = (bf16[32,2,128,128]{3,2,1,0:T(8,128)(2,1)S(1)}, bf16[32,2,128,128]{3,2,1,0:T(8,128)(2,1)}, u32[]{:S(2)}) copy-start(bf16[32,2,128,128]{3,2,1,0:T(8,128)(2,1)} %param.10) | copy-start | bytes 6291460
  7.2 137.5 %all-gather.2.cloned.1.call-start = ((), (), s32[]{:S(2)}) async-start(), calls=%async_computation.3 | async-start | bytes 12976128 | tf_op jit(solution)/shard_map/all_gather | solution.py:53
  27.5 106.0 %all-to-all-start = ((bf16[128,128,128]{2,0,1:T(8,128)(2,1)}), bf16[128,128,128]{2,0,1:T(8,128)(2,1)}, u32[]{:S(2)}, u32[]{:S(2)}) async-start(bf16[128,128,128]{2,0,1:T(8,128)(2,1)} %select_bitcast_fusion), calls=%async_computation | async-start | bytes 8388608 | tf_op jit(solution)/shard_map/all_to_all | solution.py:45
  36.7 185.3 %reduce-scatter.5.cloned.1.call-start = ((), (), s32[]{:S(2)}) async-start(), calls=%async_computation.4 | async-start | bytes 442368 | tf_op jit(solution)/shard_map/reduce_scatter | solution.py:63
  141.7 3.0 copy-start.2
  151.1 23.6 %copy-start.3 = (f32[128]{0:T(128)S(1)}, f32[128]{0:T(128)}, u32[]{:S(2)}) copy-start(f32[128]{0:T(128)} %param.11) | copy-start | bytes 1540
  184.4 157.1 %reduce-scatter.7.cloned.1.call-start = ((), (), s32[]{:S(2)}) async-start(), calls=%async_computation.5 | async-start | bytes 12976128
  210.1 131.4 %copy-start.1 = (bf16[32,2,128,128]{3,2,1,0:T(8,128)(2,1)S(1)}, bf16[32,2,128,128]{3,2,1,0:T(8,128)(2,1)}, u32[]{:S(2)}) copy-start(bf16[32,2,128,128]{3,2,1,0:T(8,128)(2,1)} %param.10) | copy-start | bytes 6291460
Sparse Core Ops, SparseCore 0:
  10.6 72.1 all-gather.1
  184.5 37.4 reduce-scatter.4
  227.2 114.1 reduce-scatter.6
where the time goes:
time: 349 us; the launch traced here: 348 us
  waiting for transfers between devices  228 us (65%)
  local copies, waits for them, and re-layouts  34 us (10%)
  matrix products  28.5 us (8%)
  blocking collectives  23.1 us (7%)
  between operations  13.9 us (4%)
  other arithmetic  11.5 us (3%)
  starting transfers between devices  9.48 us (3%)
    unnamed x4, waiting for transfers between devices  120 us
    all_to_all x1, waiting for transfers between devices, body(): lax.all_to_all(outgoing, 'vocab', split_axis=1, concat_axis=1, tiled=True)  95.5 us
    unnamed x10, local copies, waits for them, and re-layouts  20 us
    psum x1, blocking collectives, body(): lax.psum((jnp.sum(shifted, axis=1), jnp.sum(mapped, axis=1)), 'vocab')  12.2 us
    reduce_scatter x1, waiting for transfers between devices, body(): lax.psum_scatter(hidden_terms.astype(jnp.bfloat16), 'vocab', scatter_dime...  11.9 us
    pmax x1, blocking collectives, body(): row_max = lax.pmax(jnp.max(logits, axis=1), 'vocab')  10.9 us
    dot_general x1, matrix products, body(): lax.dot_general(dlogits, full_weight, (((1,), (1,)), ((), ())), preferred...  9.61 us
    all_to_all x1, starting transfers between devices, body(): lax.all_to_all(outgoing, 'vocab', split_axis=1, concat_axis=1, tiled=True)  9.18 us
  transfers between devices with their start and end apart: 4, of which 3 were waited for; matrix products, arithmetic and copies ran while one was open for 16% of the time, Pallas kernels for 0%

commit v1 on v0

v1 whole, which is shorter than its diff:
```python
import jax
import jax.numpy as jnp
from jax import lax
from jax.experimental import pallas as pl
from jax.experimental.pallas import tpu as pltpu
from jax.sharding import PartitionSpec as P

X, Y, C, Z = 4, 4, 2, 8
G = X * C
DP = X * Y * C
MESH = pl.DeviceIdType.MESH
F32 = jnp.float32
BF16 = jnp.bfloat16


def to_row(col):
    return jnp.transpose(jnp.broadcast_to(col, (128, 128)))[0:1, :]


def to_cols(row):
    return jnp.transpose(jnp.broadcast_to(row, (128, 128)))


def kernel(
    x_hbm, w_hbm, t_hbm, idx, tiles_hbm, gs_in,
    hg, wg,
    tl, tsend, tall, psend, prcv, x_all, x_t, w_all, e_ref, mp, tiles, dl,
    dwp, dwr, dxp, dsib, dxo, dxs, dxr, hsend, hr,
    gsb, gs_all, st1, st1r, st2, st2r, ms1, ms1r, ms2, ms2r, fin,
    sem_l, sem_t, sem_p, sem_x, sem_xf, sem_w, sem_g, sem_s1, sem_s2, sem_m1, sem_m2,
    sem_dw, sem_ds, sem_dx, sem_h,
):
    dp = lax.axis_index("dp")
    z = lax.axis_index("vocab")
    x = dp // (Y * C)
    y = (dp // C) % Y
    c = dp % C
    me = c * X + x
    D = x_hbm.shape[1]
    DR = w_hbm.shape[0]
    NB = tl.shape[1] // 128
    CG = w_all.shape[1]

    def dp_of(g):
        return ((g % X) * Y + y) * C + g // X

    sib = (x * Y + y) * C + (1 - c)

    load_t = pltpu.make_async_copy(t_hbm, tl, sem_l.at[0])
    load_t.start()
    load_x = pltpu.make_async_copy(x_hbm, x_all.at[me], sem_l.at[1])
    load_x.start()
    load_w = pltpu.make_async_copy(
        w_hbm.at[:, pl.ds(me * CG, CG)], w_all.at[pl.ds(dp * DR, DR)], sem_l.at[2]
    )
    load_w.start()
    load_tiles = pltpu.make_async_copy(
        tiles_hbm.at[pl.ds(me * 4, 4)], tiles, sem_l.at[3]
    )
    load_tiles.start()

    barrier = pltpu.get_barrier_semaphore()

    def greet_group(i, _):
        g = (me + i % G) % G
        pl.semaphore_signal(
            barrier, inc=1, device_id=(dp_of(g), (z + i // G) % Z), device_id_type=MESH
        )
        return 0

    lax.fori_loop(1, G * Z, greet_group, 0)

    def greet_plane(i, _):
        far = (dp + i) % DP

        @pl.when((far // C) % Y != y)
        def _():
            pl.semaphore_signal(barrier, inc=1, device_id=(far, z), device_id_type=MESH)

        return 0

    lax.fori_loop(1, DP, greet_plane, 0)

    gsb[...] = jnp.broadcast_to(gs_in[...], (8, 128))
    gs_all[me] = gsb[...]
    load_t.wait()

    def probs(zt, store):
        rows = jnp.exp(tl[pl.ds(zt * 16, 16), :]).astype(BF16)
        for j in range(NB):
            store(j, rows[:, j * 128 : (j + 1) * 128])

    def order(k):
        return 4 + (1 - 2 * (k % 2)) * ((k + 1) // 2)

    def t_copy(rz, src):
        zt = (z + rz) % Z
        return pltpu.make_async_remote_copy(
            src_ref=tsend.at[zt],
            dst_ref=tall.at[pl.ds(src * NB, NB)],
            send_sem=sem_t.at[0, rz],
            recv_sem=sem_t.at[1, rz],
            device_id=(dp, zt),
            device_id_type=MESH,
        )

    def prep(k, _):
        zt = (z + order(k)) % Z

        def store(j, v):
            tsend[zt, j] = v

        probs(zt, store)
        return 0

    lax.fori_loop(0, Z - 1, prep, 0)

    pl.semaphore_wait(barrier, (G * Z - 1) + (DP - G))

    def t_start(k, _):
        t_copy(order(k), z).start()
        return 0

    lax.fori_loop(0, Z - 1, t_start, 0)

    def x_copy(rx, src_g):
        return pltpu.make_async_remote_copy(
            src_ref=x_hbm,
            dst_ref=x_all.at[src_g],
            send_sem=sem_x.at[0, rx],
            recv_sem=sem_x.at[1, rx],
            device_id=(((x + rx) % X * Y + y) * C + c, z),
            device_id_type=MESH,
        )

    def xs_copy(rx, g, src):
        return pltpu.make_async_remote_copy(
            src_ref=src,
            dst_ref=x_all.at[g],
            send_sem=sem_xf.at[0, rx],
            recv_sem=sem_xf.at[1, rx],
            device_id=(sib, z),
            device_id_type=MESH,
        )

    for rx in (2, 1, 3):
        x_copy(rx, me).start()
    xs_copy(0, me, x_hbm).start()

    def g_copy(r, src_g):
        return pltpu.make_async_remote_copy(
            src_ref=gsb,
            dst_ref=gs_all.at[src_g],
            send_sem=sem_g.at[0, r],
            recv_sem=sem_g.at[1, r],
            device_id=(dp_of((me + r) % G), z),
            device_id_type=MESH,
        )

    def g_start(r, _):
        g_copy(r, me).start()
        return 0

    lax.fori_loop(1, G, g_start, 0)

    def w_copy(r, src_dp):
        far = (dp + r) % DP
        gf = (far % C) * X + far // (Y * C)
        return pltpu.make_async_remote_copy(
            src_ref=w_hbm.at[:, pl.ds(gf * CG, CG)],
            dst_ref=w_all.at[pl.ds(src_dp * DR, DR)],
            send_sem=sem_w.at[0, r],
            recv_sem=sem_w.at[1, r],
            device_id=(far, z),
            device_id_type=MESH,
        )

    def w_start(r, _):
        w_copy(r, dp).start()
        return 0

    lax.fori_loop(1, DP, w_start, 0)

    def store_own(j, v):
        tall[z * NB + j] = v

    probs(z, store_own)

    def t_wait(k, _):
        rz = order(k)
        t_copy(rz, (z + Z - rz) % Z).wait_recv()
        return 0

    lax.fori_loop(0, Z - 1, t_wait, 0)

    def p_copy(rz, rg, src_slot):
        zt = (z + rz) % Z
        g = (me + rg) % G
        return pltpu.make_async_remote_copy(
            src_ref=psend.at[zt * G + g],
            dst_ref=prcv.at[src_slot],
            send_sem=sem_p.at[0, rz * G + rg],
            recv_sem=sem_p.at[1, rz * G + rg],
            device_id=(dp_of(g), zt),
            device_id_type=MESH,
        )

    def pick(zt, g, store):
        base = zt * (G * 8) + g * 8
        for p in range(8):
            store(p, tall[idx[base + p]])

    def pick_send(i, _):
        rz = order(i // G)
        rg = i % G
        zt = (z + rz) % Z
        g = (me + rg) % G

        def store(p, v):
            psend[zt * G + g, p] = v

        pick(zt, g, store)
        p_copy(rz, rg, me * Z + z).start()
        return 0

    lax.fori_loop(0, (Z - 1) * G, pick_send, 0)

    def pick_send_here(rg, _):
        g = (me + rg) % G

        def store(p, v):
            psend[z * G + g, p] = v

        pick(z, g, store)
        p_copy(0, rg, me * Z + z).start()
        return 0

    lax.fori_loop(1, G, pick_send_here, 0)

    def store_mine(p, v):
        prcv[me * Z + z, p] = v

    pick(z, me, store_mine)

    load_x.wait()
    for rx in (1, 3, 2):
        src = c * X + (x + X - rx) % X
        x_copy(rx, src).wait_recv()
        xs_copy(rx, src, x_all.at[src]).start()

    def x_turn(r, _):
        x_t[:, pl.ds(pl.multiple_of(r * 128, 128), 128)] = jnp.transpose(x_all[r])
        return 0

    for rx in range(X):
        xs_copy(rx, (1 - c) * X + (x + X - rx) % X, x_hbm).wait_recv()
    lax.fori_loop(0, G, x_turn, 0)

    load_w.wait()

    def w_wait(r, _):
        w_copy(r, (dp + DP - r) % DP).wait_recv()
        return 0

    lax.fori_loop(1, DP, w_wait, 0)

    def logits(r, _):
        l = jnp.dot(x_all[r], w_all[...], preferred_element_type=F32)
        m = jnp.max(l, axis=1, keepdims=True)
        e = jnp.exp(l - m)
        e_ref[r] = e
        st1[0, pl.ds(r, 1), :] = to_row(m)
        st1[1, pl.ds(r, 1), :] = to_row(jnp.sum(e, axis=1, keepdims=True))
        return 0

    lax.fori_loop(0, G, logits, 0)

    def group_copy(src, dst, sems, r):
        return pltpu.make_async_remote_copy(
            src_ref=src,
            dst_ref=dst.at[r],
            send_sem=sems.at[0, r],
            recv_sem=sems.at[1, r],
            device_id=(dp_of((me + r) % G), z),
            device_id_type=MESH,
        )

    def z_copy(src, dst, sems, r):
        return pltpu.make_async_remote_copy(
            src_ref=src,
            dst_ref=dst.at[r],
            send_sem=sems.at[0, r],
            recv_sem=sems.at[1, r],
            device_id=(dp, (z + r) % Z),
            device_id_type=MESH,
        )

    def swap(copy, src, dst, sems, n):
        def start(r, _):
            copy(src, dst, sems, r).start()
            return 0

        lax.fori_loop(1, n, start, 0)

        def wait(r, _):
            copy(src, dst, sems, r).wait_recv()
            return 0

        lax.fori_loop(1, n, wait, 0)

    def merge(own, came, n, out):
        top = own[0]
        for r in range(1, n):
            top = jnp.maximum(top, came[r, 0])
        total = own[1] * jnp.exp(own[0] - top)
        for r in range(1, n):
            total = total + came[r, 1] * jnp.exp(came[r, 0] - top)
        out[0] = top
        out[1] = total

    swap(group_copy, st1, st1r, sem_s1, G)
    merge(st1, st1r, G, st2)
    swap(z_copy, st2, st2r, sem_s2, Z)
    merge(st2, st2r, Z, fin)

    def g_wait(r, _):
        g_copy(r, (me + G - r) % G).wait_recv()
        return 0

    lax.fori_loop(1, G, g_wait, 0)

    load_tiles.wait()

    def p_wait(i, _):
        rz = i // G
        rg = i % G
        p_copy(rz, rg, ((me + G - rg) % G) * Z + (z + Z - rz) % Z).wait_recv()
        return 0

    lax.fori_loop(1, G * Z, p_wait, 0)

    def mapping(r, _):
        total = jnp.zeros((128, 1), F32)
        for b in range(4):
            first = prcv[pl.ds(r * Z, Z), 2 * b].reshape(128, 128)
            second = prcv[pl.ds(r * Z, Z), 2 * b + 1].reshape(128, 128)
            m = jnp.dot(
                jnp.concatenate([first, second], axis=1), tiles[b], preferred_element_type=F32
            )
            mp[r, :, b * 128 : (b + 1) * 128] = m
            total = total + jnp.sum(m, axis=1, keepdims=True)
        ms1[pl.ds(r, 1), :] = to_row(total)
        return 0

    lax.fori_loop(0, G, mapping, 0)

    swap(group_copy, ms1, ms1r, sem_m1, G)
    mass = ms1[...]
    for r in range(1, G):
        mass = mass + ms1r[r]
    ms2[...] = mass
    swap(z_copy, ms2, ms2r, sem_m2, Z)
    mass = ms2[...]
    for r in range(1, Z):
        mass = mass + ms2r[r]
    ms1r[0] = mass * jnp.exp(st1[0] - fin[0]) / fin[1]

    def grads(r, _):
        gs_row = gs_all[r, 0:1, :]
        scale = to_cols(gs_row)
        coef = to_cols(gs_row * ms1r[0, pl.ds(r, 1), :])
        for b in range(4):
            cols = slice(b * 128, (b + 1) * 128)
            dl[pl.ds(pl.multiple_of(r * 128, 128), 128), cols] = (
                coef * e_ref[r, :, cols] - scale * mp[r, :, cols]
            ).astype(BF16)
        return 0

    lax.fori_loop(0, G, grads, 0)

    NC = D // 512
    HALF = X * 128

    def ds_copy(n):
        cols = pl.ds(pl.multiple_of(n * 512, 512), 512)
        return pltpu.make_async_remote_copy(
            src_ref=dxp.at[:, cols],
            dst_ref=dsib.at[:, cols],
            send_sem=sem_ds.at[0, n],
            recv_sem=sem_ds.at[1, n],
            device_id=(sib, z),
            device_id_type=MESH,
        )

    def dx_part(core, n):
        rows = pl.ds(pl.multiple_of(core * HALF, HALF), HALF)
        return lax.dot_general(
            dl[rows, :],
            w_all[pl.ds(pl.multiple_of(n * 512, 512), 512), :],
            (((1,), (1,)), ((), ())),
            preferred_element_type=F32,
        )

    def dx_other(n, _):
        dxp[:, pl.ds(pl.multiple_of(n * 512, 512), 512)] = dx_part(1 - c, n).astype(BF16)
        ds_copy(n).start()
        return 0

    lax.fori_loop(0, NC, dx_other, 0)

    def dx_copy(rx, n):
        cols = pl.ds(pl.multiple_of(n * 512, 512), 512)
        xt = (x + rx) % X
        return pltpu.make_async_remote_copy(
            src_ref=dxs.at[pl.ds(pl.multiple_of(xt * 128, 128), 128), cols],
            dst_ref=dxr.at[rx - 1, :, cols],
            send_sem=sem_dx.at[0, (rx - 1) * NC + n],
            recv_sem=sem_dx.at[1, (rx - 1) * NC + n],
            device_id=((xt * Y + y) * C + c, z),
            device_id_type=MESH,
        )

    def dx_mine(n, _):
        cols = pl.ds(pl.multiple_of(n * 512, 512), 512)
        dxo[:, cols] = dx_part(c, n)
        return 0

    lax.fori_loop(0, NC, dx_mine, 0)

    def dx_join(n, _):
        cols = pl.ds(pl.multiple_of(n * 512, 512), 512)
        ds_copy(n).wait_recv()
        dxs[:, cols] = (dxo[:, cols] + dsib[:, cols].astype(F32)).astype(BF16)
        for rx in (2, 1, 3):
            dx_copy(rx, n).start()
        return 0

    lax.fori_loop(0, NC, dx_join, 0)

    PER = 8
    NQ = DP // PER

    def dw_copy(far, src_y, src_g, r):
        return pltpu.make_async_remote_copy(
            src_ref=dwp.at[pl.ds(far * DR, DR)],
            dst_ref=dwr.at[src_y, :, pl.ds(src_g * CG, CG)],
            send_sem=sem_dw.at[0, r],
            recv_sem=sem_dw.at[1, r],
            device_id=(far, z),
            device_id_type=MESH,
        )

    keep_dw = pltpu.make_async_copy(
        dwp.at[pl.ds(dp * DR, DR)], dwr.at[y, :, pl.ds(me * CG, CG)], sem_l.at[4]
    )

    def dw_part(i, _):
        q = (dp // PER + 1 + i) % NQ
        rows = pl.ds(pl.multiple_of(q * (PER * DR), PER * DR), PER * DR)
        dwp[rows, :] = jnp.dot(x_t[rows, :], dl[...], preferred_element_type=F32).astype(BF16)

        def send(k, _):
            far = q * PER + (dp + k) % PER

            @pl.when(far != dp)
            def _():
                dw_copy(far, y, me, (far - dp + DP) % DP).start()

            return 0

        lax.fori_loop(0, PER, send, 0)
        return 0

    lax.fori_loop(0, NQ, dw_part, 0)
    keep_dw.start()

    def dx_wait(i, _):
        dx_copy(i // NC + 1, i % NC).wait_recv()
        return 0

    lax.fori_loop(0, (X - 1) * NC, dx_wait, 0)
    for r4 in range(4):
        own = pl.ds(pl.multiple_of(x * 128 + r4 * 32, 32), 32)
        sub = slice(r4 * 32, (r4 + 1) * 32)
        total = dxs[own, :].astype(F32)
        for k in range(X - 1):
            total = total + dxr[k, sub, :].astype(F32)
        for k in range(Z):
            hsend[k, sub, :] = total[:, k * 192 : (k + 1) * 192].astype(BF16)

    def h_copy(r):
        zt = (z + r) % Z
        return pltpu.make_async_remote_copy(
            src_ref=hsend.at[zt],
            dst_ref=hr.at[r],
            send_sem=sem_h.at[0, r],
            recv_sem=sem_h.at[1, r],
            device_id=(dp, zt),
            device_id_type=MESH,
        )

    def h_start(k, _):
        h_copy(order(k)).start()
        return 0

    lax.fori_loop(0, Z - 1, h_start, 0)

    keep_dw.wait()

    def dw_wait(r, _):
        src = (dp + DP - r) % DP
        dw_copy((dp + r) % DP, (src // C) % Y, (src % C) * X + src // (Y * C), r).wait_recv()
        return 0

    lax.fori_loop(1, DP, dw_wait, 0)

    def dw_sum(k, _):
        cols = pl.ds(pl.multiple_of(k * 512, 512), 512)
        total = dwr[0, :, cols].astype(F32)
        for k2 in range(1, Y):
            total = total + dwr[k2, :, cols].astype(F32)
        wg[:, cols] = total.astype(BF16)
        return 0

    lax.fori_loop(0, G, dw_sum, 0)

    def h_wait(r, _):
        h_copy(r).wait_recv()
        return 0

    lax.fori_loop(1, Z, h_wait, 0)
    total = hsend[z].astype(F32)
    for r in range(1, Z):
        total = total + hr[r].astype(F32)
    hg[...] = total.astype(BF16)

    def done_z(r, _):
        t_copy(r, z).wait_send()
        z_copy(st2, st2r, sem_s2, r).wait_send()
        z_copy(ms2, ms2r, sem_m2, r).wait_send()
        h_copy(r).wait_send()
        return 0

    lax.fori_loop(1, Z, done_z, 0)

    def done_g(r, _):
        g_copy(r, me).wait_send()
        group_copy(st1, st1r, sem_s1, r).wait_send()
        group_copy(ms1, ms1r, sem_m1, r).wait_send()
        return 0

    lax.fori_loop(1, G, done_g, 0)

    def done_p(i, _):
        p_copy(i // G, i % G, me * Z + z).wait_send()
        return 0

    lax.fori_loop(1, G * Z, done_p, 0)

    def done_w(r, _):
        w_copy(r, dp).wait_send()
        dw_copy((dp + r) % DP, y, me, r).wait_send()
        return 0

    lax.fori_loop(1, DP, done_w, 0)
    for rx in range(1, X):
        x_copy(rx, me).wait_send()
    for rx in range(X):
        xs_copy(rx, me, x_hbm).wait_send()

    def done_ds(n, _):
        ds_copy(n).wait_send()
        return 0

    lax.fori_loop(0, NC, done_ds, 0)

    def done_dx(i, _):
        dx_copy(i // NC + 1, i % NC).wait_send()
        return 0

    lax.fori_loop(0, (X - 1) * NC, done_dx, 0)


def body(student_hidden, head_weight, teacher_logprobs, align_index, align_tiles, grad_scale):
    T, D = student_hidden.shape
    DR, V = head_weight.shape
    VT = teacher_logprobs.shape[1]
    NB = VT // 128
    CG = V // G
    tiles = align_tiles.reshape(align_tiles.shape[0], 256, 128)
    sem = lambda n: pltpu.SemaphoreType.DMA((2, n))
    vm = pltpu.VMEM
    anywhere = pl.BlockSpec(memory_space=pl.ANY)
    in_vmem = pl.BlockSpec(memory_space=pltpu.VMEM)
    return pl.pallas_call(
        kernel,
        out_shape=(
            jax.ShapeDtypeStruct((T, D // Z), BF16),
            jax.ShapeDtypeStruct((DR, V), BF16),
        ),
        in_specs=[
            anywhere, anywhere, anywhere,
            pl.BlockSpec(memory_space=pltpu.SMEM),
            anywhere, in_vmem,
        ],
        out_specs=(in_vmem, in_vmem),
        scratch_shapes=[
            vm((T, VT), F32),
            vm((Z, NB, 16, 128), BF16),
            vm((Z * NB, 16, 128), BF16),
            vm((Z * G, 8, 16, 128), BF16),
            vm((Z * G, 8, 16, 128), BF16),
            vm((G, T, D), BF16),
            vm((D, G * T), BF16),
            vm((D, CG), BF16),
            vm((G, T, CG), F32),
            vm((G, T, CG), F32),
            vm((4, 256, 128), BF16),
            vm((G * T, CG), BF16),
            vm((D, CG), BF16),
            vm((Y, DR, V), BF16),
            vm((X * T, D), BF16),
            vm((X * T, D), BF16),
            vm((X * T, D), F32),
            vm((X * T, D), BF16),
            vm((X - 1, T, D), BF16),
            vm((Z, T, D // Z), BF16),
            vm((Z, T, D // Z), BF16),
            vm((8, 128), F32),
            vm((G, 8, 128), F32),
            vm((2, 8, 128), F32),
            vm((G, 2, 8, 128), F32),
            vm((2, 8, 128), F32),
            vm((Z, 2, 8, 128), F32),
            vm((8, 128), F32),
            vm((G, 8, 128), F32),
            vm((8, 128), F32),
            vm((Z, 8, 128), F32),
            vm((2, 8, 128), F32),
            pltpu.SemaphoreType.DMA((5,)),
            sem(Z), sem(Z * G), sem(X), sem(X), sem(DP), sem(G), sem(G), sem(Z), sem(G), sem(Z),
            sem(DP), sem(D // 512), sem((X - 1) * (D // 512)), sem(Z),
        ],
        compiler_params=pltpu.CompilerParams(
            collective_id=0, has_side_effects=True, vmem_limit_bytes=56 * 2**20
        ),
        name="distill_backward",
    )(
        student_hidden, head_weight, teacher_logprobs, align_index.reshape(-1), tiles,
        grad_scale.reshape(1, T),
    )


def solution(mesh):
    placed = (
        P("dp", None),
        P("dp", "vocab"),
        P("dp", "vocab"),
        P(),
        P("vocab", None, None, None),
        P("dp"),
    )
    return jax.shard_map(
        body,
        mesh=mesh,
        in_specs=placed,
        out_specs=(P("dp", "vocab"), P("dp", "vocab")),
        check_vma=False,
    )
```

time: 349 us -> 159 us (0.46)
  waiting for transfers between devices: 228 us -> 0 us
  Pallas kernels: 0 us -> 153 us
  local copies, waits for them, and re-layouts: 34 us -> 4.86 us
  matrix products: 28.5 us -> 0 us
  blocking collectives: 23.1 us -> 0 us
  between operations: 13.9 us -> 0.65 us
  other arithmetic: 11.5 us -> 0 us
  starting transfers between devices: 9.48 us -> 0 us
    pallas_call x0 -> x1, Pallas kernels: none -> 153 us  [body(): pl.pallas_call(kernel, out_shape=(jax.ShapeDtypeStruct((T, D // Z), BF16)...]
    unnamed x4 -> x0, waiting for transfers between devices: 120 us -> none
    all_to_all x1 -> x0, waiting for transfers between devices: 95.5 us -> none  [body(): lax.all_to_all(outgoing, 'vocab', split_axis=1, concat_axis=1, tiled=True)]
    dot_general x4 -> x0, matrix products: 28.5 us -> none  [the longest x1 9.61 us: body(): lax.dot_general(dlogits, full_weight, (((1,), (1,)), ((), ())), preferred...]
    unnamed x10 -> x2, local copies, waits for them, and re-layouts: 20 us -> 2.57 us
    psum x1 -> x0, blocking collectives: 12.2 us -> none  [body(): lax.psum((jnp.sum(shifted, axis=1), jnp.sum(mapped, axis=1)), 'vocab')]
    reduce_scatter x1 -> x0, waiting for transfers between devices: 11.9 us -> none  [body(): lax.psum_scatter(hidden_terms.astype(jnp.bfloat16), 'vocab', scatter_dime...]
    pmax x1 -> x0, blocking collectives: 10.9 us -> none  [body(): row_max = lax.pmax(jnp.max(logits, axis=1), 'vocab')]
  transfers between devices with their start and end apart: 4 -> 0, of which waited for: 3 -> 0; matrix products, arithmetic and copies ran while one was open for 16% -> 0% of each run, Pallas kernels for 0% -> 0%
where the time goes in v1:
time: 159 us
  Pallas kernels  153 us (96%)
  local copies, waits for them, and re-layouts  4.86 us (3%)
    pallas_call x1, Pallas kernels, body(): pl.pallas_call(kernel, out_shape=(jax.ShapeDtypeStruct((T, D // Z), BF16)...  153 us

profile of v1, /device:TPU:1, one launch (start us, length us, event | category | flops | bytes accessed | tf_op | source)
XLA Modules:
  0.0 158.6 jit_solution(1167506553878352015)
XLA Ops:
  0.6 0.8 copy.9
  1.4 0.7 reshape.13.idx
  2.2 153.1 %distill_backward.1 = (bf16[128,192]{1,0:T(8,128)(2,1)}, bf16[48,4096]{1,0:T(8,128)(2,1)}) custom-call(bf16[128,1536]{1,0:T(8,128)(2,1)} %x_hbm.1, bf16[48,4096]{1,0:T(8,128)(2,1)} %w_hbm.1, f32[128,5120]{1,0:T(8,128)} %t_hbm.1, s32[512]{0:T(512)} %reshape.13.idx, bf16[32,256,128]{2,1,0:T(8,128)(2,1)} %bitcast.2, f32[1,128]{1,0:T(1,128)} %bitcast.3), custom_call_target="tpu_custom_call" | custom-call | tf_op jit(solution)/shard_map/distill_backward/pallas_call | solution.py:595
  155.3 1.6 copy.10
  156.9 1.8 %copy.12 = bf16[48,4096]{1,0:T(8,128)(2,1)} copy(bf16[48,4096]{1,0:T(8,128)(2,1)} %get-tuple-element.9) | data formatting | bytes 786432

commit v2 on v1

v2 whole, which is shorter than its diff:
```python
import jax
import jax.numpy as jnp
from jax import lax
from jax.experimental import pallas as pl
from jax.experimental.pallas import tpu as pltpu
from jax.sharding import PartitionSpec as P

X, Y, C, Z = 4, 4, 2, 8
G = X * C
DP = X * Y * C
MESH = pl.DeviceIdType.MESH
F32 = jnp.float32
BF16 = jnp.bfloat16


def to_row(col):
    return jnp.transpose(jnp.broadcast_to(col, (128, 128)))[0:1, :]


def to_cols(row):
    return jnp.transpose(jnp.broadcast_to(row, (128, 128)))


def kernel(
    x_hbm, w_hbm, t_hbm, idx, tiles_hbm, gs_in,
    hg, wg,
    tl, tsend, tall, psend, prcv, x_all, x_t, w_all, e_ref, tiles, dl,
    dwa, dwp, dwy, dws, dwr, dxp, dsib, dxo, dxs, dxr, hsend, hr,
    st1, st1r, st2, st2r, fin, rs_own, rs_z, rs_all, ms1, ms1r, mg, mg_all,
    sem_l, sem_t, sem_p, sem_x, sem_xf, sem_w, sem_wy, sem_s1, sem_s2, sem_r1, sem_r2, sem_m1, sem_m2,
    sem_dw, sem_dwy, sem_ds, sem_dx, sem_h,
):
    dp = lax.axis_index("dp")
    z = lax.axis_index("vocab")
    x = dp // (Y * C)
    y = (dp // C) % Y
    c = dp % C
    me = x * C + c
    D = x_hbm.shape[1]
    DR = w_hbm.shape[0]
    NB = tl.shape[1] // 128
    CG = w_all.shape[1]

    def dp_of(g):
        return ((g // C) * Y + y) * C + g % C

    sib = (x * Y + y) * C + (1 - c)

    load_t = pltpu.make_async_copy(t_hbm, tl, sem_l.at[0])
    load_t.start()
    load_x = pltpu.make_async_copy(x_hbm, x_all.at[me], sem_l.at[1])
    load_x.start()
    load_w = pltpu.make_async_copy(
        w_hbm.at[:, pl.ds(me * CG, CG)], w_all.at[pl.ds(dp * DR, DR)], sem_l.at[2]
    )
    load_w.start()
    load_tiles = pltpu.make_async_copy(
        tiles_hbm.at[pl.ds(me * 4, 4)], tiles, sem_l.at[3]
    )
    load_tiles.start()

    barrier = pltpu.get_barrier_semaphore()

    def greet_group(i, _):
        g = (me + i % G) % G
        pl.semaphore_signal(
            barrier, inc=1, device_id=(dp_of(g), (z + i // G) % Z), device_id_type=MESH
        )
        return 0

    lax.fori_loop(1, G * Z, greet_group, 0)

    for ry in range(1, Y):
        pl.semaphore_signal(
            barrier,
            inc=1,
            device_id=((x * Y + (y + ry) % Y) * C + c, z),
            device_id_type=MESH,
        )

    load_t.wait()

    def probs(zt, store):
        rows = jnp.exp(tl[pl.ds(zt * 16, 16), :]).astype(BF16)
        for j in range(NB):
            store(j, rows[:, j * 128 : (j + 1) * 128])

    def order(k):
        return 4 + (1 - 2 * (k % 2)) * ((k + 1) // 2)

    def t_copy(rz, src):
        zt = (z + rz) % Z
        return pltpu.make_async_remote_copy(
            src_ref=tsend.at[zt],
            dst_ref=tall.at[pl.ds(src * NB, NB)],
            send_sem=sem_t.at[0, rz],
            recv_sem=sem_t.at[1, rz],
            device_id=(dp, zt),
            device_id_type=MESH,
        )

    def prep(k, _):
        zt = (z + order(k)) % Z

        def store(j, v):
            tsend[zt, j] = v

        probs(zt, store)
        return 0

    lax.fori_loop(0, Z - 1, prep, 0)

    load_tiles.wait()
    ones = jnp.ones((8, 128), BF16)
    for p in range(8):
        tile = tiles[p // 2, (p % 2) * 128 : (p % 2 + 1) * 128, :]
        sums = lax.dot_general(
            ones, tile, (((1,), (1,)), ((), ())), preferred_element_type=F32
        )
        rs_own[p : p + 1, :] = sums[0:1, :]

    pl.semaphore_wait(barrier, (G * Z - 1) + (Y - 1))

    def rz_copy(r, src):
        zt = (z + r) % Z
        return pltpu.make_async_remote_copy(
            src_ref=rs_own,
            dst_ref=rs_z.at[src],
            send_sem=sem_r1.at[0, r],
            recv_sem=sem_r1.at[1, r],
            device_id=(dp, zt),
            device_id_type=MESH,
        )

    def rg_copy(r, src):
        return pltpu.make_async_remote_copy(
            src_ref=rs_z,
            dst_ref=rs_all.at[src],
            send_sem=sem_r2.at[0, r],
            recv_sem=sem_r2.at[1, r],
            device_id=(dp_of((me + r) % G), z),
            device_id_type=MESH,
        )

    def rz_start(r, _):
        rz_copy(r, z).start()
        return 0

    lax.fori_loop(1, Z, rz_start, 0)
    rs_z[z] = rs_own[...]

    def t_start(k, _):
        t_copy(order(k), z).start()
        return 0

    lax.fori_loop(0, Z - 1, t_start, 0)

    def w_copy(r, src_dp):
        g = (me + r) % G
        return pltpu.make_async_remote_copy(
            src_ref=w_hbm.at[:, pl.ds(g * CG, CG)],
            dst_ref=w_all.at[pl.ds(src_dp * DR, DR)],
            send_sem=sem_w.at[0, r],
            recv_sem=sem_w.at[1, r],
            device_id=(dp_of(g), z),
            device_id_type=MESH,
        )

    def w_start(r, _):
        w_copy(r, dp).start()
        return 0

    lax.fori_loop(1, G, w_start, 0)

    def wy_copy(i, back):
        ry = i // X + 1
        xs = i % X
        src_y = (y + Y - ry) % Y if back else y
        rows = pl.ds((xs * Y + src_y) * (C * DR), C * DR)
        return pltpu.make_async_remote_copy(
            src_ref=w_all.at[rows],
            dst_ref=w_all.at[rows],
            send_sem=sem_wy.at[0, i],
            recv_sem=sem_wy.at[1, i],
            device_id=((x * Y + (y + ry) % Y) * C + c, z),
            device_id_type=MESH,
        )

    def x_copy(rx, src_g):
        return pltpu.make_async_remote_copy(
            src_ref=x_hbm,
            dst_ref=x_all.at[src_g],
            send_sem=sem_x.at[0, rx],
            recv_sem=sem_x.at[1, rx],
            device_id=(((x + rx) % X * Y + y) * C + c, z),
            device_id_type=MESH,
        )

    def xs_copy(rx, g, src):
        return pltpu.make_async_remote_copy(
            src_ref=src,
            dst_ref=x_all.at[g],
            send_sem=sem_xf.at[0, rx],
            recv_sem=sem_xf.at[1, rx],
            device_id=(sib, z),
            device_id_type=MESH,
        )

    for rx in (2, 1, 3):
        x_copy(rx, me).start()
    xs_copy(0, me, x_hbm).start()

    def store_own(j, v):
        tall[z * NB + j] = v

    probs(z, store_own)

    def rz_wait(r, _):
        rz_copy(r, (z + Z - r) % Z).wait_recv()
        return 0

    lax.fori_loop(1, Z, rz_wait, 0)
    rs_all[me] = rs_z[...]

    def rg_start(r, _):
        rg_copy(r, me).start()
        return 0

    lax.fori_loop(1, G, rg_start, 0)

    load_w.wait()

    def w_wait(r, _):
        w_copy(r, dp_of((me + G - r) % G)).wait_recv()
        return 0

    lax.fori_loop(1, G, w_wait, 0)

    def wy_start(i, _):
        wy_copy(i, 0).start()
        return 0

    lax.fori_loop(0, (Y - 1) * X, wy_start, 0)

    load_x.wait()
    for rx in (1, 3, 2):
        src = (x + X - rx) % X * C + c
        x_copy(rx, src).wait_recv()
        xs_copy(rx, src, x_all.at[src]).start()

    def x_turn(r, _):
        x_t[:, pl.ds(pl.multiple_of(r * 128, 128), 128)] = jnp.transpose(x_all[r])
        return 0

    for rx in range(X):
        xs_copy(rx, (x + X - rx) % X * C + 1 - c, x_hbm).wait_recv()
    lax.fori_loop(0, G, x_turn, 0)

    def wy_wait(i, _):
        wy_copy(i, 1).wait_recv()
        return 0

    lax.fori_loop(0, (Y - 1) * X, wy_wait, 0)

    def logits(r, _):
        l = jnp.dot(x_all[r], w_all[...], preferred_element_type=F32)
        m = jnp.max(l, axis=1, keepdims=True)
        e = jnp.exp(l - m)
        e_ref[r] = e
        st1[0, pl.ds(r, 1), :] = to_row(m)
        st1[1, pl.ds(r, 1), :] = to_row(jnp.sum(e, axis=1, keepdims=True))
        return 0

    lax.fori_loop(0, G, logits, 0)

    def group_copy(src, dst, sems, r):
        return pltpu.make_async_remote_copy(
            src_ref=src,
            dst_ref=dst.at[r],
            send_sem=sems.at[0, r],
            recv_sem=sems.at[1, r],
            device_id=(dp_of((me + r) % G), z),
            device_id_type=MESH,
        )

    def z_copy(src, dst, sems, r):
        return pltpu.make_async_remote_copy(
            src_ref=src,
            dst_ref=dst.at[r],
            send_sem=sems.at[0, r],
            recv_sem=sems.at[1, r],
            device_id=(dp, (z + r) % Z),
            device_id_type=MESH,
        )

    def swap(copy, src, dst, sems, n):
        def start(r, _):
            copy(src, dst, sems, r).start()
            return 0

        lax.fori_loop(1, n, start, 0)

        def wait(r, _):
            copy(src, dst, sems, r).wait_recv()
            return 0

        lax.fori_loop(1, n, wait, 0)

    def merge(own, came, n, out):
        top = own[0]
        for r in range(1, n):
            top = jnp.maximum(top, came[r, 0])
        total = own[1] * jnp.exp(own[0] - top)
        for r in range(1, n):
            total = total + came[r, 1] * jnp.exp(came[r, 0] - top)
        out[0] = top
        out[1] = total

    swap(group_copy, st1, st1r, sem_s1, G)
    merge(st1, st1r, G, st2)
    def sz_start(r, _):
        z_copy(st2, st2r, sem_s2, r).start()
        return 0

    lax.fori_loop(1, Z, sz_start, 0)

    def rg_wait(r, _):
        rg_copy(r, (me + G - r) % G).wait_recv()
        return 0

    lax.fori_loop(1, G, rg_wait, 0)

    def t_wait(k, _):
        rz = order(k)
        t_copy(rz, (z + Z - rz) % Z).wait_recv()
        return 0

    lax.fori_loop(0, Z - 1, t_wait, 0)

    def p_copy(i, back):
        sign = 1 - 2 * back
        g = (x + X + sign * (i // 16 + 1)) % X * C + (c + i % 2) % C
        zt = (z + Z + sign * order(i // 2 % 8)) % Z
        return pltpu.make_async_remote_copy(
            src_ref=psend.at[zt * G + g],
            dst_ref=prcv.at[g * Z + zt if back else me * Z + z],
            send_sem=sem_p.at[0, i],
            recv_sem=sem_p.at[1, i],
            device_id=(dp_of(g), zt),
            device_id_type=MESH,
        )

    def weigh(i, acc):
        g = i % G
        zt = i // G
        for p in range(8):
            acc = acc + tall[idx[i * 8 + p]].astype(F32) * rs_all[g, zt, p : p + 1, :]
        return acc

    acc = lax.fori_loop(0, G * Z, weigh, jnp.zeros((16, 128), F32))

    own_mass = jnp.broadcast_to(jnp.sum(acc, axis=1, keepdims=True), (16, 128))
    lane = lax.broadcasted_iota(jnp.int32, (16, 128), 1)
    row = lax.broadcasted_iota(jnp.int32, (16, 128), 0)
    placed = jnp.sum(jnp.where(lane == row + z * 16, own_mass, 0.0), axis=0, keepdims=True)
    ms1[...] = jnp.broadcast_to(placed, (8, 128))

    def mz_start(r, _):
        z_copy(ms1, ms1r, sem_m1, r).start()
        return 0

    lax.fori_loop(1, Z, mz_start, 0)

    SELF = (X - 1) * 16 + 14

    def pick(i, store):
        g = (x + i // 16 + 1) % X * C + (c + i % 2) % C
        zt = (z + order(i // 2 % 8)) % Z
        base = zt * (G * 8) + g * 8
        for p in range(8):
            store(zt * G + g, p, tall[idx[base + p]])

    def pick_send(i, _):
        def store(slot, p, v):
            psend[slot, p] = v

        @pl.when(i != SELF)
        def _():
            pick(i, store)
            p_copy(i, 0).start()

        return 0

    def store_mine(slot, p, v):
        prcv[me * Z + z, p] = v

    lax.fori_loop(0, 16, pick_send, 0)
    pick(SELF, store_mine)

    def mz_wait(r, _):
        z_copy(ms1, ms1r, sem_m1, r).wait_recv()
        return 0

    lax.fori_loop(1, Z, mz_wait, 0)
    mass = ms1[...]
    for r in range(1, Z):
        mass = mass + ms1r[r]
    top_row = lax.broadcasted_iota(jnp.int32, (8, 128), 0) == 0
    mg[...] = jnp.where(top_row, mass, jnp.broadcast_to(gs_in[...], (8, 128)))

    def mg_copy(r, src):
        return pltpu.make_async_remote_copy(
            src_ref=mg,
            dst_ref=mg_all.at[src],
            send_sem=sem_m2.at[0, r],
            recv_sem=sem_m2.at[1, r],
            device_id=(dp_of((me + r) % G), z),
            device_id_type=MESH,
        )

    def mg_start(r, _):
        mg_copy(r, me).start()
        return 0

    lax.fori_loop(1, G, mg_start, 0)
    mg_all[me] = mg[...]

    lax.fori_loop(16, 32, pick_send, 0)

    def sz_wait(r, _):
        z_copy(st2, st2r, sem_s2, r).wait_recv()
        return 0

    lax.fori_loop(1, Z, sz_wait, 0)
    merge(st2, st2r, Z, fin)


    def mg_wait(r, _):
        mg_copy(r, (me + G - r) % G).wait_recv()
        return 0

    lax.fori_loop(1, G, mg_wait, 0)
    for r in range(G):
        st1r[0, 0, r : r + 1, :] = mg_all[r, 0:1, :] * mg_all[r, 1:2, :]
    fin[1] = st1r[0, 0] * jnp.exp(st1[0] - fin[0]) / fin[1]

    NC = D // 512
    PAIR = C * 128

    def ds_copy(k):
        return pltpu.make_async_remote_copy(
            src_ref=dxp.at[k],
            dst_ref=dsib.at[k],
            send_sem=sem_ds.at[0, k],
            recv_sem=sem_ds.at[1, k],
            device_id=(sib, z),
            device_id_type=MESH,
        )

    def dx_copy(k):
        return pltpu.make_async_remote_copy(
            src_ref=dxs.at[k],
            dst_ref=dxr.at[k],
            send_sem=sem_dx.at[0, k],
            recv_sem=sem_dx.at[1, k],
            device_id=(((x + X - k) % X * Y + y) * C + c, z),
            device_id_type=MESH,
        )

    def step(s):
        k = (s + 1) % X
        xs = (x + X - k) % X
        pair = pl.ds(pl.multiple_of(xs * PAIR, PAIR), PAIR)

        def p_wait(i, _):
            @pl.when(s * 16 + i != SELF)
            def _():
                p_copy(s * 16 + i, 1).wait_recv()

            return 0

        lax.fori_loop(0, 16, p_wait, 0)

        @pl.when(s + 2 < X)
        def _():
            lax.fori_loop((s + 2) * 16, (s + 3) * 16, pick_send, 0)

        for cc in range(C):
            r = xs * C + cc
            scale = to_cols(mg_all[r, 1:2, :])
            coef = to_cols(fin[1, pl.ds(r, 1), :])
            for b in range(4):
                first = prcv[pl.ds(r * Z, Z), 2 * b].reshape(128, 128)
                second = prcv[pl.ds(r * Z, Z), 2 * b + 1].reshape(128, 128)
                m = jnp.dot(
                    jnp.concatenate([first, second], axis=1),
                    tiles[b],
                    preferred_element_type=F32,
                )
                cols = slice(b * 128, (b + 1) * 128)
                dl[pl.ds(pl.multiple_of(r * 128, 128), 128), cols] = (
                    coef * e_ref[r, :, cols] - scale * m
                ).astype(BF16)
        for n in range(NC):
            cols = slice(n * 512, (n + 1) * 512)
            dxo[:, cols] = lax.dot_general(
                dl[pair, :], w_all[cols, :], (((1,), (1,)), ((), ())),
                preferred_element_type=F32,
            )
        dxp[k] = dxo[pl.ds(pl.multiple_of((1 - c) * 128, 128), 128), :].astype(BF16)
        ds_copy(k).start()

    def join(k):
        ds_copy(k).wait_recv()
        dxs[k] = (
            dxo[pl.ds(pl.multiple_of(c * 128, 128), 128), :] + dsib[k].astype(F32)
        ).astype(BF16)

    def dw_sums(k, rows):
        pair = pl.ds(pl.multiple_of((x + X - k) % X * PAIR, PAIR), PAIR)
        return jnp.dot(x_t[rows, pair], dl[pair, :], preferred_element_type=F32)

    dwa[...] = jnp.zeros_like(dwa)

    def early(i, _):
        step(i)

        def add(q, _):
            rows = pl.ds(pl.multiple_of(q * 384, 384), 384)
            dwa[rows, :] += dw_sums(i + 1, rows)
            return 0

        lax.fori_loop(0, D // 384, add, 0)
        join(i + 1)
        dx_copy(i + 1).start()
        return 0

    lax.fori_loop(0, X - 1, early, 0)
    step(X - 1)

    YR = C * DR

    def wy_rows(q, yt):
        return pl.ds((q * Y + yt) * YR, YR)

    def dwy_copy(q, ry):
        yt = (y + ry) % Y
        return pltpu.make_async_remote_copy(
            src_ref=dwp.at[wy_rows(q, yt)],
            dst_ref=dwy.at[ry - 1, q],
            send_sem=sem_dwy.at[0, ry - 1, q],
            recv_sem=sem_dwy.at[1, ry - 1, q],
            device_id=((x * Y + yt) * C + c, z),
            device_id_type=MESH,
        )

    def dw_part(i):
        q = (x + 1 + i) % X
        rows = pl.ds(pl.multiple_of(q * (Y * YR), Y * YR), Y * YR)
        total = dwa[rows, :] + dw_sums(0, rows)
        dwa[rows, :] = total
        dwp[rows, :] = total.astype(BF16)
        for ry in (2, 1, 3):
            dwy_copy(q, ry).start()

    def dw_copy(r, src_g):
        g = (me + r) % G
        return pltpu.make_async_remote_copy(
            src_ref=dws.at[g // C, pl.ds(g % C * DR, DR)],
            dst_ref=dwr.at[src_g],
            send_sem=sem_dw.at[0, r],
            recv_sem=sem_dw.at[1, r],
            device_id=(dp_of(g), z),
            device_id_type=MESH,
        )

    dw_part(0)

    join(0)

    def dx_wait(k, _):
        dx_copy(k).wait_recv()
        return 0

    lax.fori_loop(1, X, dx_wait, 0)
    for r4 in range(4):
        sub = slice(r4 * 32, (r4 + 1) * 32)
        total = dxs[0, sub, :].astype(F32)
        for k in range(1, X):
            total = total + dxr[k, sub, :].astype(F32)
        for k in range(Z):
            hsend[k, sub, :] = total[:, k * 192 : (k + 1) * 192].astype(BF16)

    def h_copy(r):
        zt = (z + r) % Z
        return pltpu.make_async_remote_copy(
            src_ref=hsend.at[zt],
            dst_ref=hr.at[r],
            send_sem=sem_h.at[0, r],
            recv_sem=sem_h.at[1, r],
            device_id=(dp, zt),
            device_id_type=MESH,
        )

    def h_start(k, _):
        h_copy(order(k)).start()
        return 0

    lax.fori_loop(0, Z - 1, h_start, 0)

    def dw_rest(i, _):
        dw_part(i)
        return 0

    lax.fori_loop(1, X, dw_rest, 0)

    def dw_join(i, _):
        q = (x + 1 + i) % X
        for ry in range(1, Y):
            dwy_copy(q, ry).wait_recv()
        total = dwa[wy_rows(q, y), :]
        for ry in range(1, Y):
            total = total + dwy[ry - 1, q].astype(F32)
        dws[q] = total.astype(BF16)
        for cc in range(C):
            r = (q * C + cc + G - me) % G

            @pl.when(r != 0)
            def _():
                dw_copy(r, me).start()

        return 0

    lax.fori_loop(0, X, dw_join, 0)
    dwr[me] = dws[x, pl.ds(pl.multiple_of(c * DR, 16), DR), :]

    def dw_wait(r, _):
        dw_copy(r, (me + G - r) % G).wait_recv()
        return 0

    lax.fori_loop(1, G, dw_wait, 0)
    for g in range(G):
        wg[:, g * CG : (g + 1) * CG] = dwr[g]

    def h_wait(r, _):
        h_copy(r).wait_recv()
        return 0

    lax.fori_loop(1, Z, h_wait, 0)
    total = hsend[z].astype(F32)
    for r in range(1, Z):
        total = total + hr[r].astype(F32)
    hg[...] = total.astype(BF16)

    def done_z(r, _):
        t_copy(r, z).wait_send()
        z_copy(st2, st2r, sem_s2, r).wait_send()
        z_copy(ms1, ms1r, sem_m1, r).wait_send()
        rz_copy(r, z).wait_send()
        h_copy(r).wait_send()
        return 0

    lax.fori_loop(1, Z, done_z, 0)

    def done_g(r, _):
        group_copy(st1, st1r, sem_s1, r).wait_send()
        rg_copy(r, me).wait_send()
        w_copy(r, dp).wait_send()
        dw_copy(r, me).wait_send()
        mg_copy(r, me).wait_send()
        return 0

    lax.fori_loop(1, G, done_g, 0)

    def done_p(i, _):
        @pl.when(i != SELF)
        def _():
            p_copy(i, 0).wait_send()

        return 0

    lax.fori_loop(0, G * Z, done_p, 0)

    def done_dw(q, _):
        for ry in range(1, Y):
            dwy_copy(q, ry).wait_send()
        return 0

    lax.fori_loop(0, X, done_dw, 0)
    for rx in range(1, X):
        x_copy(rx, me).wait_send()
    for rx in range(X):
        xs_copy(rx, me, x_hbm).wait_send()

    def done_wy(i, _):
        wy_copy(i, 0).wait_send()
        return 0

    lax.fori_loop(0, (Y - 1) * X, done_wy, 0)

    def done_ds(k, _):
        ds_copy(k).wait_send()
        return 0

    lax.fori_loop(0, X, done_ds, 0)

    def done_dx(k, _):
        dx_copy(k).wait_send()
        return 0

    lax.fori_loop(1, X, done_dx, 0)


def body(student_hidden, head_weight, teacher_logprobs, align_index, align_tiles, grad_scale):
    T, D = student_hidden.shape
    DR, V = head_weight.shape
    VT = teacher_logprobs.shape[1]
    NB = VT // 128
    CG = V // G
    tiles = align_tiles.reshape(align_tiles.shape[0], 256, 128)
    sem = lambda n: pltpu.SemaphoreType.DMA((2, n))
    vm = pltpu.VMEM
    anywhere = pl.BlockSpec(memory_space=pl.ANY)
    in_vmem = pl.BlockSpec(memory_space=pltpu.VMEM)
    return pl.pallas_call(
        kernel,
        out_shape=(
            jax.ShapeDtypeStruct((T, D // Z), BF16),
            jax.ShapeDtypeStruct((DR, V), BF16),
        ),
        in_specs=[
            anywhere, anywhere, anywhere,
            pl.BlockSpec(memory_space=pltpu.SMEM),
            anywhere, in_vmem,
        ],
        out_specs=(in_vmem, in_vmem),
        scratch_shapes=[
            vm((T, VT), F32),
            vm((Z, NB, 16, 128), BF16),
            vm((Z * NB, 16, 128), BF16),
            vm((Z * G, 8, 16, 128), BF16),
            vm((Z * G, 8, 16, 128), BF16),
            vm((G, T, D), BF16),
            vm((D, G * T), BF16),
            vm((D, CG), BF16),
            vm((G, T, CG), F32),
            vm((4, 256, 128), BF16),
            vm((G * T, CG), BF16),
            vm((D, CG), F32),
            vm((D, CG), BF16),
            vm((Y - 1, X, C * DR, CG), BF16),
            vm((X, C * DR, CG), BF16),
            vm((G, DR, CG), BF16),
            vm((X, T, D), BF16),
            vm((X, T, D), BF16),
            vm((C * T, D), F32),
            vm((X, T, D), BF16),
            vm((X, T, D), BF16),
            vm((Z, T, D // Z), BF16),
            vm((Z, T, D // Z), BF16),
            vm((2, 8, 128), F32),
            vm((G, 2, 8, 128), F32),
            vm((2, 8, 128), F32),
            vm((Z, 2, 8, 128), F32),
            vm((2, 8, 128), F32),
            vm((8, 128), F32),
            vm((Z, 8, 128), F32),
            vm((G, Z, 8, 128), F32),
            vm((8, 128), F32),
            vm((Z, 8, 128), F32),
            vm((8, 128), F32),
            vm((G, 8, 128), F32),
            pltpu.SemaphoreType.DMA((4,)),
            sem(Z), sem(Z * G), sem(X), sem(X), sem(G), sem((Y - 1) * X), sem(G), sem(Z), sem(Z), sem(G), sem(Z), sem(G),
            sem(G), pltpu.SemaphoreType.DMA((2, Y - 1, X)), sem(X), sem(X), sem(Z),
        ],
        compiler_params=pltpu.CompilerParams(
            collective_id=0, has_side_effects=True, vmem_limit_bytes=56 * 2**20
        ),
        name="distill_backward",
    )(
        student_hidden, head_weight, teacher_logprobs, align_index.reshape(-1), tiles,
        grad_scale.reshape(1, T),
    )


def solution(mesh):
    placed = (
        P("dp", None),
        P("dp", "vocab"),
        P("dp", "vocab"),
        P(),
        P("vocab", None, None, None),
        P("dp"),
    )
    return jax.shard_map(
        body,
        mesh=mesh,
        in_specs=placed,
        out_specs=(P("dp", "vocab"), P("dp", "vocab")),
        check_vma=False,
    )
```

time: 159 us -> 136 us (0.86)
  Pallas kernels: 153 us -> 130 us
    pallas_call x1, Pallas kernels: 153 us -> 130 us  [body(): pl.pallas_call(kernel, out_shape=(jax.ShapeDtypeStruct((T, D // Z), BF16)...]
where the time goes in v2:
time: 136 us
  Pallas kernels  130 us (96%)
  local copies, waits for them, and re-layouts  4.86 us (4%)
    pallas_call x1, Pallas kernels, body(): pl.pallas_call(kernel, out_shape=(jax.ShapeDtypeStruct((T, D // Z), BF16)...  130 us

profile of v2, /device:TPU:1, one launch (start us, length us, event | category | flops | bytes accessed | tf_op | source)
XLA Modules:
  0.0 136.0 jit_solution(5261515865911059355)
XLA Ops:
  0.6 0.8 copy.9
  1.4 0.7 reshape.13.idx
  2.2 130.5 %distill_backward.1 = (bf16[128,192]{1,0:T(8,128)(2,1)}, bf16[48,4096]{1,0:T(8,128)(2,1)}) custom-call(bf16[128,1536]{1,0:T(8,128)(2,1)} %x_hbm.1, bf16[48,4096]{1,0:T(8,128)(2,1)} %w_hbm.1, f32[128,5120]{1,0:T(8,128)} %t_hbm.1, s32[512]{0:T(512)} %reshape.13.idx, bf16[32,256,128]{2,1,0:T(8,128)(2,1)} %bitcast.2, f32[1,128]{1,0:T(1,128)} %bitcast.3), custom_call_target="tpu_custom_call" | custom-call | tf_op jit(solution)/shard_map/distill_backward/pallas_call | solution.py:725
  132.6 1.6 %copy.10 = bf16[128,192]{0,1:T(8,128)(2,1)} copy(bf16[128,192]{1,0:T(8,128)(2,1)} %get-tuple-element.4) | data formatting | bytes 98304 | tf_op jit(solution)/shard_map/distill_backward/pallas_call | solution.py:725
  134.2 1.8 %copy.12 = bf16[48,4096]{1,0:T(8,128)(2,1)} copy(bf16[48,4096]{1,0:T(8,128)(2,1)} %get-tuple-element.9) | data formatting | bytes 786432

commit v3 on v2

--- a/solution.py
+++ b/solution.py
@@ -6,6 +6,7 @@
 from jax.sharding import PartitionSpec as P
 
 X, Y, C, Z = 4, 4, 2, 8
+K = 2
 G = X * C
 DP = X * Y * C
 MESH = pl.DeviceIdType.MESH
@@ -25,7 +26,7 @@
     x_hbm, w_hbm, t_hbm, idx, tiles_hbm, gs_in,
     hg, wg,
     tl, tsend, tall, psend, prcv, x_all, x_t, w_all, e_ref, tiles, dl,
-    dwa, dwp, dwy, dws, dwr, dxp, dsib, dxo, dxs, dxr, hsend, hr,
+    dwa, dwp, way, way_sum, dwy, dws, dwr, dxp, dsib, dxo, dxs, dxr, hsend, hr,
     st1, st1r, st2, st2r, fin, rs_own, rs_z, rs_all, ms1, ms1r, mg, mg_all,
     sem_l, sem_t, sem_p, sem_x, sem_xf, sem_w, sem_wy, sem_s1, sem_s2, sem_r1, sem_r2, sem_m1, sem_m2,
     sem_dw, sem_dwy, sem_ds, sem_dx, sem_h,
@@ -248,31 +249,6 @@
         x_copy(rx, src).wait_recv()
         xs_copy(rx, src, x_all.at[src]).start()
 
-    def x_turn(r, _):
-        x_t[:, pl.ds(pl.multiple_of(r * 128, 128), 128)] = jnp.transpose(x_all[r])
-        return 0
-
-    for rx in range(X):
-        xs_copy(rx, (x + X - rx) % X * C + 1 - c, x_hbm).wait_recv()
-    lax.fori_loop(0, G, x_turn, 0)
-
-    def wy_wait(i, _):
-        wy_copy(i, 1).wait_recv()
-        return 0
-
-    lax.fori_loop(0, (Y - 1) * X, wy_wait, 0)
-
-    def logits(r, _):
-        l = jnp.dot(x_all[r], w_all[...], preferred_element_type=F32)
-        m = jnp.max(l, axis=1, keepdims=True)
-        e = jnp.exp(l - m)
-        e_ref[r] = e
-        st1[0, pl.ds(r, 1), :] = to_row(m)
-        st1[1, pl.ds(r, 1), :] = to_row(jnp.sum(e, axis=1, keepdims=True))
-        return 0
-
-    lax.fori_loop(0, G, logits, 0)
-
     def group_copy(src, dst, sems, r):
         return pltpu.make_async_remote_copy(
             src_ref=src,
@@ -292,19 +268,6 @@
             device_id=(dp, (z + r) % Z),
             device_id_type=MESH,
         )
-
-    def swap(copy, src, dst, sems, n):
-        def start(r, _):
-            copy(src, dst, sems, r).start()
-            return 0
-
-        lax.fori_loop(1, n, start, 0)
-
-        def wait(r, _):
-            copy(src, dst, sems, r).wait_recv()
-            return 0
-
-        lax.fori_loop(1, n, wait, 0)
 
     def merge(own, came, n, out):
         top = own[0]
@@ -316,14 +279,6 @@
         out[0] = top
         out[1] = total
 
-    swap(group_copy, st1, st1r, sem_s1, G)
-    merge(st1, st1r, G, st2)
-    def sz_start(r, _):
-        z_copy(st2, st2r, sem_s2, r).start()
-        return 0
-
-    lax.fori_loop(1, Z, sz_start, 0)
-
     def rg_wait(r, _):
         rg_copy(r, (me + G - r) % G).wait_recv()
         return 0
@@ -354,7 +309,7 @@
         g = i % G
         zt = i // G
         for p in range(8):
-            acc = acc + tall[idx[i * 8 + p]].astype(F32) * rs_all[g, zt, p : p + 1, :]
+            acc = acc + tall[idx[p % K, i * 4 + p // K]].astype(F32) * rs_all[g, zt, p : p + 1, :]
         return acc
 
     acc = lax.fori_loop(0, G * Z, weigh, jnp.zeros((16, 128), F32))
@@ -376,9 +331,9 @@
     def pick(i, store):
         g = (x + i // 16 + 1) % X * C + (c + i % 2) % C
         zt = (z + order(i // 2 % 8)) % Z
-        base = zt * (G * 8) + g * 8
+        base = zt * (G * 4) + g * 4
         for p in range(8):
-            store(zt * G + g, p, tall[idx[base + p]])
+            store(zt * G + g, p, tall[idx[p % K, base + p // K]])
 
     def pick_send(i, _):
         def store(slot, p, v):
@@ -394,8 +349,40 @@
     def store_mine(slot, p, v):
         prcv[me * Z + z, p] = v
 
-    lax.fori_loop(0, 16, pick_send, 0)
+    lax.fori_loop(0, 8, pick_send, 0)
     pick(SELF, store_mine)
+
+    for rx in range(X):
+        xs_copy(rx, (x + X - rx) % X * C + 1 - c, x_hbm).wait_recv()
+
+    def wy_wait(i, _):
+        wy_copy(i, 1).wait_recv()
+        return 0
+
+    lax.fori_loop(0, (Y - 1) * X, wy_wait, 0)
+
+    def logits(r, _):
+        both = jnp.dot(
+            x_all[pl.ds(2 * r, 2)].reshape(256, D), w_all[...], preferred_element_type=F32
+        )
+        for h in range(2):
+            l = both[h * 128 : (h + 1) * 128]
+            m = jnp.max(l, axis=1, keepdims=True)
+            e = jnp.exp(l - m)
+            e_ref[2 * r + h] = e
+            st1[0, pl.ds(2 * r + h, 1), :] = to_row(m)
+            st1[1, pl.ds(2 * r + h, 1), :] = to_row(jnp.sum(e, axis=1, keepdims=True))
+        return 0
+
+    lax.fori_loop(0, G // 2, logits, 0)
+
+    def s_start(r, _):
+        group_copy(st1, st1r, sem_s1, r).start()
+        return 0
+
+    lax.fori_loop(1, G, s_start, 0)
+    lax.fori_loop(8, 16, pick_send, 0)
+
 
     def mz_wait(r, _):
         z_copy(ms1, ms1r, sem_m1, r).wait_recv()
@@ -425,7 +412,25 @@
     lax.fori_loop(1, G, mg_start, 0)
     mg_all[me] = mg[...]
 
+    def s_wait(r, _):
+        group_copy(st1, st1r, sem_s1, r).wait_recv()
+        return 0
+
+    lax.fori_loop(1, G, s_wait, 0)
+    merge(st1, st1r, G, st2)
+
+    def sz_start(r, _):
+        z_copy(st2, st2r, sem_s2, r).start()
+        return 0
+
+    lax.fori_loop(1, Z, sz_start, 0)
     lax.fori_loop(16, 32, pick_send, 0)
+
+    def x_turn(r, _):
+        x_t[:, pl.ds(pl.multiple_of(r * 128, 128), 128)] = jnp.transpose(x_all[r])
+        return 0
+
+    lax.fori_loop(0, G, x_turn, 0)
 
     def sz_wait(r, _):
         z_copy(st2, st2r, sem_s2, r).wait_recv()
@@ -467,10 +472,9 @@
             device_id_type=MESH,
         )
 
-    def step(s):
+    def step_map(s):
         k = (s + 1) % X
         xs = (x + X - k) % X
-        pair = pl.ds(pl.multiple_of(xs * PAIR, PAIR), PAIR)
 
         def p_wait(i, _):
             @pl.when(s * 16 + i != SELF)
@@ -501,6 +505,10 @@
                 dl[pl.ds(pl.multiple_of(r * 128, 128), 128), cols] = (
                     coef * e_ref[r, :, cols] - scale * m
                 ).astype(BF16)
+
+    def step_dx(s):
+        k = (s + 1) % X
+        pair = pl.ds(pl.multiple_of((x + X - k) % X * PAIR, PAIR), PAIR)
         for n in range(NC):
             cols = slice(n * 512, (n + 1) * 512)
             dxo[:, cols] = lax.dot_general(
@@ -523,7 +531,8 @@
     dwa[...] = jnp.zeros_like(dwa)
 
     def early(i, _):
-        step(i)
+        step_map(i)
+        step_dx(i)
 
         def add(q, _):
             rows = pl.ds(pl.multiple_of(q * 384, 384), 384)
@@ -536,21 +545,46 @@
         return 0
 
     lax.fori_loop(0, X - 1, early, 0)
-    step(X - 1)
+    step_map(X - 1)
 
     YR = C * DR
 
-    def wy_rows(q, yt):
-        return pl.ds((q * Y + yt) * YR, YR)
-
-    def dwy_copy(q, ry):
-        yt = (y + ry) % Y
-        return pltpu.make_async_remote_copy(
-            src_ref=dwp.at[wy_rows(q, yt)],
-            dst_ref=dwy.at[ry - 1, q],
-            send_sem=sem_dwy.at[0, ry - 1, q],
-            recv_sem=sem_dwy.at[1, ry - 1, q],
-            device_id=((x * Y + yt) * C + c, z),
+    def next_y(d):
+        return (y + 1 + d * (Y - 2)) % Y
+
+    def to_y(d):
+        return ((x * Y + next_y(d)) * C + c, z)
+
+    def half(q, yt, h):
+        return pl.ds((q * Y + yt) * YR + h * DR, DR)
+
+    def way_copy(q, d):
+        return pltpu.make_async_remote_copy(
+            src_ref=dwp.at[half(q, (y + 2) % Y, d)],
+            dst_ref=way.at[d, q],
+            send_sem=sem_dwy.at[0, d, q],
+            recv_sem=sem_dwy.at[1, d, q],
+            device_id=to_y(d),
+            device_id_type=MESH,
+        )
+
+    def plain_copy(q, d):
+        return pltpu.make_async_remote_copy(
+            src_ref=dwp.at[half(q, next_y(d), 1 - d)],
+            dst_ref=dwy.at[d, q, 1 - d],
+            send_sem=sem_dwy.at[0, 2 + d, q],
+            recv_sem=sem_dwy.at[1, 2 + d, q],
+            device_id=to_y(d),
+            device_id_type=MESH,
+        )
+
+    def sum_copy(q, d):
+        return pltpu.make_async_remote_copy(
+            src_ref=way_sum.at[d, q],
+            dst_ref=dwy.at[d, q, d],
+            send_sem=sem_dwy.at[0, 4 + d, q],
+            recv_sem=sem_dwy.at[1, 4 + d, q],
+            device_id=to_y(d),
             device_id_type=MESH,
         )
 
@@ -560,8 +594,10 @@
         total = dwa[rows, :] + dw_sums(0, rows)
         dwa[rows, :] = total
         dwp[rows, :] = total.astype(BF16)
-        for ry in (2, 1, 3):
-            dwy_copy(q, ry).start()
+        for d in range(2):
+            way_copy(q, d).start()
+        for d in range(2):
+            plain_copy(q, d).start()
 
     def dw_copy(r, src_g):
         g = (me + r) % G
@@ -574,7 +610,13 @@
             device_id_type=MESH,
         )
 
-    dw_part(0)
+    def dw_rest(i, _):
+        dw_part(i)
+        return 0
+
+    lax.fori_loop(0, 2, dw_rest, 0)
+    step_dx(X - 1)
+    lax.fori_loop(2, X, dw_rest, 0)
 
     join(0)
 
@@ -608,20 +650,28 @@
 
     lax.fori_loop(0, Z - 1, h_start, 0)
 
-    def dw_rest(i, _):
-        dw_part(i)
-        return 0
-
-    lax.fori_loop(1, X, dw_rest, 0)
+    def dw_way(i, _):
+        q = (x + 1 + i) % X
+        for d in range(2):
+            way_copy(q, d).wait_recv()
+            way_sum[d, q] = (
+                dwa[half(q, next_y(d), d), :] + way[d, q].astype(F32)
+            ).astype(BF16)
+            sum_copy(q, d).start()
+        return 0
+
+    lax.fori_loop(0, X, dw_way, 0)
 
     def dw_join(i, _):
         q = (x + 1 + i) % X
-        for ry in range(1, Y):
-            dwy_copy(q, ry).wait_recv()
-        total = dwa[wy_rows(q, y), :]
-        for ry in range(1, Y):
-            total = total + dwy[ry - 1, q].astype(F32)
-        dws[q] = total.astype(BF16)
+        for d in range(2):
+            plain_copy(q, d).wait_recv()
+            sum_copy(q, d).wait_recv()
+        for h in range(2):
+            total = dwa[half(q, y, h), :]
+            for d in range(2):
+                total = total + dwy[d, q, h].astype(F32)
+            dws[q, h * DR : (h + 1) * DR, :] = total.astype(BF16)
         for cc in range(C):
             r = (q * C + cc + G - me) % G
 
@@ -650,7 +700,7 @@
     total = hsend[z].astype(F32)
     for r in range(1, Z):
         total = total + hr[r].astype(F32)
-    hg[...] = total.astype(BF16)
+    hg[...] = jnp.transpose(total).astype(BF16)
 
     def done_z(r, _):
         t_copy(r, z).wait_send()
@@ -682,8 +732,10 @@
     lax.fori_loop(0, G * Z, done_p, 0)
 
     def done_dw(q, _):
-        for ry in range(1, Y):
-            dwy_copy(q, ry).wait_send()
+        for d in range(2):
+            way_copy(q, d).wait_send()
+            plain_copy(q, d).wait_send()
+            sum_copy(q, d).wait_send()
         return 0
 
     lax.fori_loop(0, X, done_dw, 0)
@@ -722,10 +774,10 @@
     vm = pltpu.VMEM
     anywhere = pl.BlockSpec(memory_space=pl.ANY)
     in_vmem = pl.BlockSpec(memory_space=pltpu.VMEM)
-    return pl.pallas_call(
+    hidden_grad, head_grad = pl.pallas_call(
         kernel,
         out_shape=(
-            jax.ShapeDtypeStruct((T, D // Z), BF16),
+            jax.ShapeDtypeStruct((D // Z, T), BF16),
             jax.ShapeDtypeStruct((DR, V), BF16),
         ),
         in_specs=[
@@ -748,7 +800,9 @@
             vm((G * T, CG), BF16),
             vm((D, CG), F32),
             vm((D, CG), BF16),
-            vm((Y - 1, X, C * DR, CG), BF16),
+            vm((2, X, DR, CG), BF16),
+            vm((2, X, DR, CG), BF16),
+            vm((2, X, 2, DR, CG), BF16),
             vm((X, C * DR, CG), BF16),
             vm((G, DR, CG), BF16),
             vm((X, T, D), BF16),
@@ -772,16 +826,17 @@
             vm((G, 8, 128), F32),
             pltpu.SemaphoreType.DMA((4,)),
             sem(Z), sem(Z * G), sem(X), sem(X), sem(G), sem((Y - 1) * X), sem(G), sem(Z), sem(Z), sem(G), sem(Z), sem(G),
-            sem(G), pltpu.SemaphoreType.DMA((2, Y - 1, X)), sem(X), sem(X), sem(Z),
+            sem(G), pltpu.SemaphoreType.DMA((2, 6, X)), sem(X), sem(X), sem(Z),
         ],
         compiler_params=pltpu.CompilerParams(
             collective_id=0, has_side_effects=True, vmem_limit_bytes=56 * 2**20
         ),
         name="distill_backward",
     )(
-        student_hidden, head_weight, teacher_logprobs, align_index.reshape(-1), tiles,
+        student_hidden, head_weight, teacher_logprobs, align_index.T, tiles,
         grad_scale.reshape(1, T),
     )
+    return hidden_grad.T, head_grad
 
 
 def solution(mesh):

time: 136 us -> 126 us (0.926)
  Pallas kernels: 130 us -> 122 us
  local copies, waits for them, and re-layouts: 4.86 us -> 3.19 us
    pallas_call x1, Pallas kernels: 130 us -> 122 us  [body(): pl.pallas_call(kernel, out_shape=(jax.ShapeDtypeStruct((D // Z, T), BF16)...]
    pallas_call x1 -> x0, local copies, waits for them, and re-layouts: 1.56 us -> none  [body(): pl.pallas_call(kernel, out_shape=(jax.ShapeDtypeStruct((T, D // Z), BF16)...]
where the time goes in v3:
time: 126 us
  Pallas kernels  122 us (97%)
  local copies, waits for them, and re-layouts  3.19 us (3%)
    pallas_call x1, Pallas kernels, body(): pl.pallas_call(kernel, out_shape=(jax.ShapeDtypeStruct((D // Z, T), BF16)...  122 us
    unnamed x2, local copies, waits for them, and re-layouts  3.19 us

profile of v3, /device:TPU:1, one launch (start us, length us, event | category | flops | bytes accessed | tf_op | source)
XLA Modules:
  0.0 126.0 jit_solution(2030800361183827330)
XLA Ops:
  0.6 122.2 %distill_backward.1 = (bf16[192,128]{1,0:T(8,128)(2,1)}, bf16[48,4096]{1,0:T(8,128)(2,1)}) custom-call(bf16[128,1536]{1,0:T(8,128)(2,1)} %x_hbm.1, bf16[48,4096]{1,0:T(8,128)(2,1)} %w_hbm.1, f32[128,5120]{1,0:T(8,128)} %t_hbm.1, s32[2,256]{1,0:T(2,128)} %bitcast.6, bf16[32,256,128]{2,1,0:T(8,128)(2,1)} %bitcast.4, f32[1,128]{1,0:T(1,128)} %bitcast.7), custom_call_target="tpu_custom_call" | custom-call | tf_op jit(solution)/shard_map/distill_backward/pallas_call | solution.py:777
  122.8 1.4 %copy.10 = bf16[128,192]{0,1:T(8,128)(2,1)} copy(bf16[128,192]{0,1:T(8,128)(2,1)} %bitcast.5) | data formatting | bytes 98304
  124.2 1.8 %copy.11 = bf16[48,4096]{1,0:T(8,128)(2,1)} copy(bf16[48,4096]{1,0:T(8,128)(2,1)} %get-tuple-element.9) | data formatting | bytes 786432

commit v4 on v3

--- a/solution.py
+++ b/solution.py
@@ -412,6 +412,8 @@
     lax.fori_loop(1, G, mg_start, 0)
     mg_all[me] = mg[...]
 
+    lax.fori_loop(16, 24, pick_send, 0)
+
     def s_wait(r, _):
         group_copy(st1, st1r, sem_s1, r).wait_recv()
         return 0
@@ -424,7 +426,7 @@
         return 0
 
     lax.fori_loop(1, Z, sz_start, 0)
-    lax.fori_loop(16, 32, pick_send, 0)
+    lax.fori_loop(24, 32, pick_send, 0)
 
     def x_turn(r, _):
         x_t[:, pl.ds(pl.multiple_of(r * 128, 128), 128)] = jnp.transpose(x_all[r])
@@ -545,6 +547,38 @@
         return 0
 
     lax.fori_loop(0, X - 1, early, 0)
+
+    def done_8(r, _):
+        t_copy(r, z).wait_send()
+        z_copy(st2, st2r, sem_s2, r).wait_send()
+        z_copy(ms1, ms1r, sem_m1, r).wait_send()
+        rz_copy(r, z).wait_send()
+        group_copy(st1, st1r, sem_s1, r).wait_send()
+        rg_copy(r, me).wait_send()
+        w_copy(r, dp).wait_send()
+        mg_copy(r, me).wait_send()
+        return 0
+
+    lax.fori_loop(1, Z, done_8, 0)
+
+    def done_p(i, _):
+        @pl.when(i != SELF)
+        def _():
+            p_copy(i, 0).wait_send()
+
+        return 0
+
+    lax.fori_loop(0, (X - 1) * 16, done_p, 0)
+    for rx in range(1, X):
+        x_copy(rx, me).wait_send()
+    for rx in range(X):
+        xs_copy(rx, me, x_hbm).wait_send()
+
+    def done_wy(i, _):
+        wy_copy(i, 0).wait_send()
+        return 0
+
+    lax.fori_loop(0, (Y - 1) * X, done_wy, 0)
     step_map(X - 1)
 
     YR = C * DR
@@ -649,6 +683,15 @@
         return 0
 
     lax.fori_loop(0, Z - 1, h_start, 0)
+    lax.fori_loop((X - 1) * 16, G * Z, done_p, 0)
+
+    def done_dx(k, _):
+        dx_copy(k).wait_send()
+        ds_copy(k).wait_send()
+        return 0
+
+    lax.fori_loop(1, X, done_dx, 0)
+    ds_copy(0).wait_send()
 
     def dw_way(i, _):
         q = (x + 1 + i) % X
@@ -702,34 +745,12 @@
         total = total + hr[r].astype(F32)
     hg[...] = jnp.transpose(total).astype(BF16)
 
-    def done_z(r, _):
-        t_copy(r, z).wait_send()
-        z_copy(st2, st2r, sem_s2, r).wait_send()
-        z_copy(ms1, ms1r, sem_m1, r).wait_send()
-        rz_copy(r, z).wait_send()
+    def done_h(r, _):
         h_copy(r).wait_send()
-        return 0
-
-    lax.fori_loop(1, Z, done_z, 0)
-
-    def done_g(r, _):
-        group_copy(st1, st1r, sem_s1, r).wait_send()
-        rg_copy(r, me).wait_send()
-        w_copy(r, dp).wait_send()
         dw_copy(r, me).wait_send()
-        mg_copy(r, me).wait_send()
-        return 0
-
-    lax.fori_loop(1, G, done_g, 0)
-
-    def done_p(i, _):
-        @pl.when(i != SELF)
-        def _():
-            p_copy(i, 0).wait_send()
-
-        return 0
-
-    lax.fori_loop(0, G * Z, done_p, 0)
+        return 0
+
+    lax.fori_loop(1, Z, done_h, 0)
 
     def done_dw(q, _):
         for d in range(2):
@@ -739,28 +760,6 @@
         return 0
 
     lax.fori_loop(0, X, done_dw, 0)
-    for rx in range(1, X):
-        x_copy(rx, me).wait_send()
-    for rx in range(X):
-        xs_copy(rx, me, x_hbm).wait_send()
-
-    def done_wy(i, _):
-        wy_copy(i, 0).wait_send()
-        return 0
-
-    lax.fori_loop(0, (Y - 1) * X, done_wy, 0)
-
-    def done_ds(k, _):
-        ds_copy(k).wait_send()
-        return 0
-
-    lax.fori_loop(0, X, done_ds, 0)
-
-    def done_dx(k, _):
-        dx_copy(k).wait_send()
-        return 0
-
-    lax.fori_loop(1, X, done_dx, 0)
 
 
 def body(student_hidden, head_weight, teacher_logprobs, align_index, align_tiles, grad_scale):

time: 126 us -> 124 us (0.984)
  Pallas kernels: 122 us -> 120 us
    pallas_call x1, Pallas kernels: 122 us -> 120 us  [body(): pl.pallas_call(kernel, out_shape=(jax.ShapeDtypeStruct((D // Z, T), BF16)...]
where the time goes in v4:
time: 124 us
  Pallas kernels  120 us (97%)
  local copies, waits for them, and re-layouts  3.19 us (3%)
    pallas_call x1, Pallas kernels, body(): pl.pallas_call(kernel, out_shape=(jax.ShapeDtypeStruct((D // Z, T), BF16)...  120 us
    unnamed x2, local copies, waits for them, and re-layouts  3.19 us

profile of v4, /device:TPU:1, one launch (start us, length us, event | category | flops | bytes accessed | tf_op | source)
XLA Modules:
  0.0 124.0 jit_solution(15483069579871506058)
XLA Ops:
  0.6 120.2 %distill_backward.1 = (bf16[192,128]{1,0:T(8,128)(2,1)}, bf16[48,4096]{1,0:T(8,128)(2,1)}) custom-call(bf16[128,1536]{1,0:T(8,128)(2,1)} %x_hbm.1, bf16[48,4096]{1,0:T(8,128)(2,1)} %w_hbm.1, f32[128,5120]{1,0:T(8,128)} %t_hbm.1, s32[2,256]{1,0:T(2,128)} %bitcast.6, bf16[32,256,128]{2,1,0:T(8,128)(2,1)} %bitcast.4, f32[1,128]{1,0:T(1,128)} %bitcast.7), custom_call_target="tpu_custom_call" | custom-call | tf_op jit(solution)/shard_map/distill_backward/pallas_call | solution.py:776
  120.8 1.4 %copy.10 = bf16[128,192]{0,1:T(8,128)(2,1)} copy(bf16[128,192]{0,1:T(8,128)(2,1)} %bitcast.5) | data formatting | bytes 98304
  122.2 1.8 %copy.11 = bf16[48,4096]{1,0:T(8,128)(2,1)} copy(bf16[48,4096]{1,0:T(8,128)(2,1)} %get-tuple-element.9) | data formatting | bytes 786432

commit v5 on v4

--- a/solution.py
+++ b/solution.py
@@ -414,6 +414,12 @@
 
     lax.fori_loop(16, 24, pick_send, 0)
 
+    def x_turn(r, _):
+        x_t[:, pl.ds(pl.multiple_of(r * 128, 128), 128)] = jnp.transpose(x_all[r])
+        return 0
+
+    lax.fori_loop(0, G, x_turn, 0)
+
     def s_wait(r, _):
         group_copy(st1, st1r, sem_s1, r).wait_recv()
         return 0
@@ -428,11 +434,6 @@
     lax.fori_loop(1, Z, sz_start, 0)
     lax.fori_loop(24, 32, pick_send, 0)
 
-    def x_turn(r, _):
-        x_t[:, pl.ds(pl.multiple_of(r * 128, 128), 128)] = jnp.transpose(x_all[r])
-        return 0
-
-    lax.fori_loop(0, G, x_turn, 0)
 
     def sz_wait(r, _):
         z_copy(st2, st2r, sem_s2, r).wait_recv()

time: 124 us -> 124 us (level)
  no operation moved by 1% of the time
where the time goes in v5:
time: 124 us
  Pallas kernels  120 us (97%)
  local copies, waits for them, and re-layouts  3.19 us (3%)
    pallas_call x1, Pallas kernels, body(): pl.pallas_call(kernel, out_shape=(jax.ShapeDtypeStruct((D // Z, T), BF16)...  120 us
    unnamed x2, local copies, waits for them, and re-layouts  3.19 us

profile of v5, /device:TPU:1, one launch (start us, length us, event | category | flops | bytes accessed | tf_op | source)
XLA Modules:
  0.0 124.0 jit_solution(3213260994008049440)
XLA Ops:
  0.6 120.2 %distill_backward.1 = (bf16[192,128]{1,0:T(8,128)(2,1)}, bf16[48,4096]{1,0:T(8,128)(2,1)}) custom-call(bf16[128,1536]{1,0:T(8,128)(2,1)} %x_hbm.1, bf16[48,4096]{1,0:T(8,128)(2,1)} %w_hbm.1, f32[128,5120]{1,0:T(8,128)} %t_hbm.1, s32[2,256]{1,0:T(2,128)} %bitcast.6, bf16[32,256,128]{2,1,0:T(8,128)(2,1)} %bitcast.4, f32[1,128]{1,0:T(1,128)} %bitcast.7), custom_call_target="tpu_custom_call" | custom-call | tf_op jit(solution)/shard_map/distill_backward/pallas_call | solution.py:777
  120.8 1.4 %copy.10 = bf16[128,192]{0,1:T(8,128)(2,1)} copy(bf16[128,192]{0,1:T(8,128)(2,1)} %bitcast.5) | data formatting | bytes 98304
  122.2 1.8 %copy.11 = bf16[48,4096]{1,0:T(8,128)(2,1)} copy(bf16[48,4096]{1,0:T(8,128)(2,1)} %get-tuple-element.9) | data formatting | bytes 786432

commit v6 on v5

--- a/solution.py
+++ b/solution.py
@@ -349,7 +349,7 @@
     def store_mine(slot, p, v):
         prcv[me * Z + z, p] = v
 
-    lax.fori_loop(0, 8, pick_send, 0)
+    lax.fori_loop(0, 16, pick_send, 0)
     pick(SELF, store_mine)
 
     for rx in range(X):
@@ -381,7 +381,6 @@
         return 0
 
     lax.fori_loop(1, G, s_start, 0)
-    lax.fori_loop(8, 16, pick_send, 0)
 
 
     def mz_wait(r, _):

time: 124 us -> 124 us (level)
  no operation moved by 1% of the time
where the time goes in v6:
time: 124 us
  Pallas kernels  120 us (97%)
  local copies, waits for them, and re-layouts  3.19 us (3%)
    pallas_call x1, Pallas kernels, body(): pl.pallas_call(kernel, out_shape=(jax.ShapeDtypeStruct((D // Z, T), BF16)...  120 us
    unnamed x2, local copies, waits for them, and re-layouts  3.19 us

profile of v6, /device:TPU:1, one launch (start us, length us, event | category | flops | bytes accessed | tf_op | source)
XLA Modules:
  0.0 124.1 jit_solution(12432147518946654056)
XLA Ops:
  0.6 120.3 %distill_backward.1 = (bf16[192,128]{1,0:T(8,128)(2,1)}, bf16[48,4096]{1,0:T(8,128)(2,1)}) custom-call(bf16[128,1536]{1,0:T(8,128)(2,1)} %x_hbm.1, bf16[48,4096]{1,0:T(8,128)(2,1)} %w_hbm.1, f32[128,5120]{1,0:T(8,128)} %t_hbm.1, s32[2,256]{1,0:T(2,128)} %bitcast.6, bf16[32,256,128]{2,1,0:T(8,128)(2,1)} %bitcast.4, f32[1,128]{1,0:T(1,128)} %bitcast.7), custom_call_target="tpu_custom_call" | custom-call | tf_op jit(solution)/shard_map/distill_backward/pallas_call | solution.py:776
  120.9 1.4 %copy.10 = bf16[128,192]{0,1:T(8,128)(2,1)} copy(bf16[128,192]{0,1:T(8,128)(2,1)} %bitcast.5) | data formatting | bytes 98304
  122.4 1.8 %copy.11 = bf16[48,4096]{1,0:T(8,128)(2,1)} copy(bf16[48,4096]{1,0:T(8,128)(2,1)} %get-tuple-element.9) | data formatting | bytes 786432
